TPU v7x, 128 devices: a whole 4x4x4 slice. The times are simulated.
128 devices in a mesh: tmpl: 32 (over z_hi, x, y), seg: 4 (over z_lo, core).
Axes of the slice: x: 4, y: 4, z: 4 (z_hi: 2, z_lo: 2; z = z_hi * 2 + z_lo), core: 2. Of those that a mesh axis runs over, the one named last changes fastest.
Arguments:
- spectra: bfloat16 [2, 2, 32, 8, 4096], P(None, None, 'tmpl', 'seg'), may hold values from -6 to 6
- templates: bfloat16 [2, 512, 4096], P(None, 'tmpl'), may hold values from -64 to 64
- bounds: int32 [512, 15], P('tmpl'), may hold values from 64 to 4032, as said below
- trigger_owner: int32 [8192, 1], P(('tmpl', 'seg')), may hold values from 0 to 31; in each aligned block of 64 rows (0 to 63, 64 to 127, ...) at most 4 rows name the same one
- trigger_template: int32 [8192], P(('tmpl', 'seg')), may hold values from 0 to 15
- trigger_segment: int32 [8192], P(('tmpl', 'seg')), may hold values from 0 to 1
- trigger_block: int32 [8192], P(('tmpl', 'seg')), may hold values from 0 to 1
Outputs:
- network_snr: float32 [512, 32, 8, 256], P('tmpl', None, 'seg')
- loudest: float32 [512], P('tmpl')
- chisq: float32 [8192, 128], P(('tmpl', 'seg'))
Inputs may be any that keep to these rules, and one draw needn't show every extreme that they name: `bounds`: each row rises; the first entry, the gaps between entries and 4096 minus the last entry are all 64 or more. `trigger_owner`: at most 4 triggers of one device name the same template shard; some device names some shard exactly 4 times.
All inputs are finite; a program needn't handle non-finite values.
Results may differ from a plain program's by a relative error of at most 0.0031.
Values may be sent and summed in bfloat16 or wider, within the bound.
A program may use at most 64 MiB of HBM per device.

v0:
```python
import math

import jax
import jax.numpy as jnp
from jax import lax
from jax.sharding import PartitionSpec as P

F = 4096
F0 = 10240
NSAMP = 2097152
STRIDE = 512
TIME = 256
TB = 128
NBINS = 16


TWO_PI = 2.0 * math.pi
EPSILON = 1e-06


def wave_table(first_bin, bin_count, time_count):
    freq_bins = first_bin + lax.broadcasted_iota(jnp.int32, (bin_count, time_count), 0)
    time_steps = lax.broadcasted_iota(jnp.int32, (bin_count, time_count), 1)
    turn_count = freq_bins * time_steps % (NSAMP // STRIDE) * STRIDE
    angles = turn_count.astype(jnp.float32) * (TWO_PI / NSAMP)
    return (jnp.cos(angles).astype(jnp.bfloat16), jnp.sin(angles).astype(jnp.bfloat16))


def band_split(tmpl_rows, bin_edges):
    freq_bins = jnp.arange(tmpl_rows.shape[-1], dtype=jnp.int32)
    bin_index = jnp.sum(
        (bin_edges[:, :, None] <= freq_bins[None, None, :]).astype(jnp.int32), axis=1
    )
    bin_mask = bin_index[:, None, :] == jnp.arange(NBINS, dtype=jnp.int32)[None, :, None]
    energy = tmpl_rows[:, 0] * tmpl_rows[:, 0] + tmpl_rows[:, 1] * tmpl_rows[:, 1]
    band_power = jnp.sum(jnp.where(bin_mask, energy[:, None, :], 0.0), axis=2) + EPSILON
    return (band_power, bin_mask)


def chi_square(seg_rows, tmpl_rows, bin_edges, blocks, cos_tb, sin_tb):
    band_power, bin_mask = band_split(tmpl_rows, bin_edges)
    total_power = jnp.sum(band_power, axis=1, keepdims=True)
    freq_bins = F0 + jnp.arange(tmpl_rows.shape[-1], dtype=jnp.int32)
    block_shift = blocks * cos_tb.shape[1]
    turn_count = freq_bins[None, :] * block_shift[:, None] % (NSAMP // STRIDE) * STRIDE
    angles = turn_count.astype(jnp.float32) * (TWO_PI / NSAMP)
    rot_cos = jnp.cos(angles)[:, None, :]
    rot_sin = jnp.sin(angles)[:, None, :]
    prod_re = (
        seg_rows[:, 0] * tmpl_rows[:, 0][:, None, :] + seg_rows[:, 1] * tmpl_rows[:, 1][:, None, :]
    )
    prod_im = (
        seg_rows[:, 1] * tmpl_rows[:, 0][:, None, :] - seg_rows[:, 0] * tmpl_rows[:, 1][:, None, :]
    )
    turned_re = (prod_re * rot_cos - prod_im * rot_sin).astype(jnp.bfloat16)
    turned_im = (prod_re * rot_sin + prod_im * rot_cos).astype(jnp.bfloat16)
    band_mask = bin_mask.astype(jnp.bfloat16)[:, :, None, :]
    left_re = turned_re[:, None] * band_mask
    left_im = turned_im[:, None] * band_mask
    corr_re = jnp.dot(left_re, cos_tb, preferred_element_type=jnp.float32) - jnp.dot(
        left_im, sin_tb, preferred_element_type=jnp.float32
    )
    corr_im = jnp.dot(left_re, sin_tb, preferred_element_type=jnp.float32) + jnp.dot(
        left_im, cos_tb, preferred_element_type=jnp.float32
    )
    whole_re = jnp.sum(corr_re, axis=1, keepdims=True)
    whole_im = jnp.sum(corr_im, axis=1, keepdims=True)
    weight = (band_power / total_power)[:, :, None, None]
    diff_re = corr_re - weight * whole_re
    diff_im = corr_im - weight * whole_im
    terms = (diff_re * diff_re + diff_im * diff_im) / band_power[:, :, None, None]
    return jnp.sum(terms, axis=(1, 2)) / (2.0 * (NBINS - 1))


def run_veto(seg_rows, tmpl_ids, blocks, bank, bank_edges, cos_tb, sin_tb):
    total_rows = seg_rows.shape[0]
    group_size = math.gcd(total_rows, 16)

    def one_group(inputs):
        group_seg, group_ids, group_blocks = inputs
        group_tmpl = jnp.moveaxis(jnp.take(bank, group_ids, axis=1), 1, 0).astype(jnp.float32)
        group_edges = jnp.take(bank_edges, group_ids, axis=0)
        return chi_square(
            group_seg.astype(jnp.float32), group_tmpl, group_edges, group_blocks, cos_tb, sin_tb
        )

    shaped = (
        seg_rows.reshape((total_rows // group_size, group_size) + seg_rows.shape[1:]),
        tmpl_ids.reshape(total_rows // group_size, group_size),
        blocks.reshape(total_rows // group_size, group_size),
    )
    return lax.map(one_group, shaped).reshape(total_rows, cos_tb.shape[1])


def body(
    spectra, templates, bounds, trigger_owner, trigger_template, trigger_segment, trigger_block
):
    cos_full, sin_full = wave_table(F0, F, TIME)
    cos_tb = cos_full[:, :TB]
    sin_tb = sin_full[:, :TB]
    tmpl_f32 = templates.astype(jnp.float32)
    band_power, unused_mask = band_split(jnp.moveaxis(tmpl_f32, 1, 0), bounds)
    total_power = jnp.sum(band_power, axis=1)
    tmpl_re = tmpl_f32[0][:, None, None, None, :]
    tmpl_im = tmpl_f32[1][:, None, None, None, :]
    piece_f32 = lax.all_gather(spectra, "tmpl", axis=2, tiled=True).astype(jnp.float32)
    prod_re = (piece_f32[0][None] * tmpl_re + piece_f32[1][None] * tmpl_im).astype(jnp.bfloat16)
    prod_im = (piece_f32[1][None] * tmpl_re - piece_f32[0][None] * tmpl_im).astype(jnp.bfloat16)
    corr_re = jnp.dot(prod_re, cos_full, preferred_element_type=jnp.float32) - jnp.dot(
        prod_im, sin_full, preferred_element_type=jnp.float32
    )
    corr_im = jnp.dot(prod_re, sin_full, preferred_element_type=jnp.float32) + jnp.dot(
        prod_im, cos_full, preferred_element_type=jnp.float32
    )
    network_snr = (
        jnp.sum(corr_re * corr_re + corr_im * corr_im, axis=1) / total_power[:, None, None, None]
    )
    loudest = lax.pmax(jnp.max(network_snr, axis=(1, 2, 3)), "seg")
    owners = trigger_owner[:, 0]
    own_rows = jnp.moveaxis(spectra[:, :, 0], 2, 0)
    picked = jnp.take(own_rows, trigger_segment, axis=0)
    bank, bank_edges = (
        lax.all_gather(templates, "tmpl", axis=1, tiled=True),
        lax.all_gather(bounds, "tmpl", axis=0, tiled=True),
    )
    tmpl_ids = owners * templates.shape[1] + trigger_template
    chisq = run_veto(picked, tmpl_ids, trigger_block, bank, bank_edges, cos_tb, sin_tb)
    return (network_snr, loudest, chisq)


def solution(mesh):
    in_specs = (
        P(None, None, "tmpl", "seg", None),
        P(None, "tmpl", None),
        P("tmpl", None),
        P(("tmpl", "seg"), None),
        P(("tmpl", "seg")),
        P(("tmpl", "seg")),
        P(("tmpl", "seg")),
    )
    out_specs = (P("tmpl", None, "seg", None), P("tmpl"), P(("tmpl", "seg"), None))
    return jax.shard_map(body, mesh=mesh, in_specs=in_specs, out_specs=out_specs, check_vma=False)
```

profile of v0, /device:TPU:0, one launch (start us, length us, event | category | flops | bytes accessed | tf_op | source)
XLA Modules:
  0.0 363.0 jit_solution(15596514872930150078)
XLA Ops:
  7.9 1.9 copy.31
  12.3 6.7 %gather_fusion.2 = bf16[64,2,2,4096]{3,2,1,0:T(2,128)(2,1)} fusion(bf16[2,2,2,4096]{3,2,1,0:T(2,128)(2,1)S(1)} %bitcast.107, s32[1024]{0:T(1024)S(1)} %pad_clamp_fusion.1), kind=kCustom, calls=%fused_computation.2 | custom fusion | bytes 4194560 | tf_op jit(solution)/shard_map/jit(_take)/gather | solution.py:121
  19.0 2.9 copy.30
  22.3 19.7 %sine_convert_fusion = (bf16[4096,256]{1,0:T(8,128)(2,1)S(1)}, bf16[4096,256]{1,0:T(8,128)(2,1)S(1)}) fusion(s32[4096]{0:T(1024)S(1)} %iota_add_fusion.1), kind=kLoop, calls=%fused_computation.112 | loop fusion | flops 17825792 | bytes 4210688 | tf_op jit(solution)/shard_map/convert_element_type | solution.py:26
  41.9 1.1 slice.92
  44.1 98.2 %all_gather.11 = s32[512,15]{1,0:T(8,128)S(1)} all-gather(s32[16,15]{1,0:T(8,128)S(1)} %copy-done.2), channel_id=1, replica_groups=mesh['tmpl'=32,'seg'=4] {'tmpl'}, dimensions={0}, use_global_device_ids=true | all-gather | bytes 31680 | tf_op jit(solution)/shard_map/all_gather | solution.py:124
  143.8 1.7 broadcast_select_fusion.2
  145.5 3.6 convert_element_type.114
  149.4 1.2 copy.27
  150.6 1.2 copy.26
  151.8 26.6 %fusion.51 = f32[16,2,32,2,256]{4,2,3,1,0:T(8,128)S(1)} fusion(f32[16,4096]{1,0:T(8,128)S(1)} %get-tuple-element.216, f32[2,32,2,4096]{3,1,2,0:T(8,128)S(1)} %copy.27, f32[16,4096]{1,0:T(8,128)S(1)} %get-tuple-element.215, f32[2,32,2,4096]{3,1,2,0:T(8,128)S(1)} %copy.26, s32[4096]{0:T(1024)S(1)} %iota_add_fusion.1), kind=kOutput, calls=%fused_computation.83 | convolution fusion | flops 4345298944 | bytes 6832128 | tf_op jit(solution)/shard_map/dot_general | solution.py:112
  178.4 25.9 %fusion.53 = f32[16,2,32,2,256]{4,2,3,1,0:T(8,128)S(1)} fusion(f32[16,4096]{1,0:T(8,128)S(1)} %get-tuple-element.216, f32[2,32,2,4096]{3,1,2,0:T(8,128)S(1)} %copy.27, f32[16,4096]{1,0:T(8,128)S(1)} %get-tuple-element.215, f32[2,32,2,4096]{3,1,2,0:T(8,128)S(1)} %copy.26, s32[4096]{0:T(1024)S(1)} %iota_add_fusion.1), kind=kOutput, calls=%fused_computation.85 | convolution fusion | flops 4345298944 | bytes 6832128 | tf_op jit(solution)/shard_map/dot_general | solution.py:112
  204.3 27.0 %fusion.52 = f32[16,2,32,2,256]{4,2,3,1,0:T(8,128)} fusion(f32[16,4096]{1,0:T(8,128)S(1)} %get-tuple-element.216, f32[2,32,2,4096]{3,1,2,0:T(8,128)S(1)} %copy.27, f32[16,4096]{1,0:T(8,128)S(1)} %get-tuple-element.215, f32[2,32,2,4096]{3,1,2,0:T(8,128)S(1)} %copy.26, s32[4096]{0:T(1024)S(1)} %iota_add_fusion.1), kind=kOutput, calls=%fused_computation.84 | convolution fusion | flops 4345298944 | bytes 6832128 | tf_op jit(solution)/shard_map/dot_general | solution.py:109
  231.3 27.9 %add_reduce_fusion = f32[16,32,2,256]{3,1,2,0:T(8,128)S(1)} fusion(f32[16,2,32,2,256]{4,2,3,1,0:T(8,128)S(1)} %fusion.51, f32[16,2,32,2,256]{4,2,3,1,0:T(8,128)S(1)} %fusion.53, f32[16,2,32,2,256]{4,2,3,1,0:T(8,128)} %fusion.52, f32[16,4096]{1,0:T(8,128)S(1)} %get-tuple-element.216, f32[2,32,2,4096]{3,1,2,0:T(8,128)S(1)} %copy.27, ...), kind=kOutput, calls=%fused_computation.125 | convolution fusion | flops 4348182528 | bytes 12075008 | tf_op jit(solution)/shard_map/dot_general | solution.py:109
  259.5 1.8 copy.33
  261.3 6.4 %pmax.7 = f32[16]{0:T(128)} all-reduce(f32[16]{0:T(128)S(1)} %get-tuple-element.200), channel_id=1, replica_groups=mesh['tmpl'=32,'seg'=4] {'seg'}, use_global_device_ids=true, to_apply=%region_5.6 | all-reduce | flops 16 | bytes 128 | tf_op jit(solution)/shard_map/pmax | solution.py:118
  267.7 87.9 %while.13 = (s32[]{:T(128)}, f32[4,16,128]{2,1,0:T(8,128)S(1)}, bf16[4,16,2,2,4096]{4,1,0,3,2:T(8,128)(2,1)}, s32[4,16]{1,0:T(4,128)S(1)}, bf16[2,512,4096]{2,0,...) while((s32[]{:T(128)}, f32[4,16,128]{2,1,0:T(8,128)S(1)}, ...), condition=%wide.region_13.14_spmd.clone, body=%wide.region_6.13_spmd.clone.sunk | while | flops 2168272896 | bytes 32583116 | solution.py:92
  267.7 4.5 %gather_fusion = bf16[16,2,4096]{2,1,0:T(2,128)(2,1)S(1)} fusion(bf16[2,512,4096]{2,0,1:T(2,128)(2,1)} %get-tuple-element.322, s32[1024]{0:T(1024)S(1)} %pad_clamp_fusion.3), kind=kCustom, calls=%fused_computation.clone.1 | custom fusion | bytes 524352 | tf_op jit(solution)/shard_map/while/body/eval_jaxpr/jit(_take)/gather | solution.py:81
  275.6 1.1 fusion.146
  276.8 1.2 constant_dynamic-slice_fusion.4
  278.7 1.1 fusion.148
  280.1 1.2 fusion.150
  281.4 3.2 fusion.151
  284.6 2.5 fusion.152
  287.1 2.6 fusion.153
  289.7 4.5 %gather_fusion = bf16[16,2,4096]{2,1,0:T(2,128)(2,1)S(1)} fusion(bf16[2,512,4096]{2,0,1:T(2,128)(2,1)} %get-tuple-element.322, s32[1024]{0:T(1024)S(1)} %pad_clamp_fusion.3), kind=kCustom, calls=%fused_computation.clone.1 | custom fusion | bytes 524352 | tf_op jit(solution)/shard_map/while/body/eval_jaxpr/jit(_take)/gather | solution.py:81
  297.6 1.1 fusion.146
  298.7 1.2 constant_dynamic-slice_fusion.4
  300.6 1.1 fusion.148
  302.1 1.2 fusion.150
  303.3 3.2 fusion.151
  306.6 2.5 fusion.152
  309.0 2.6 fusion.153
  311.7 4.5 %gather_fusion = bf16[16,2,4096]{2,1,0:T(2,128)(2,1)S(1)} fusion(bf16[2,512,4096]{2,0,1:T(2,128)(2,1)} %get-tuple-element.322, s32[1024]{0:T(1024)S(1)} %pad_clamp_fusion.3), kind=kCustom, calls=%fused_computation.clone.1 | custom fusion | bytes 524352 | tf_op jit(solution)/shard_map/while/body/eval_jaxpr/jit(_take)/gather | solution.py:81
  319.6 1.1 fusion.146
  320.7 1.2 constant_dynamic-slice_fusion.4
  322.6 1.1 fusion.148
  324.1 1.2 fusion.150
  325.3 3.2 fusion.151
  328.5 2.5 fusion.152
  331.0 2.6 fusion.153
  333.6 4.5 %gather_fusion = bf16[16,2,4096]{2,1,0:T(2,128)(2,1)S(1)} fusion(bf16[2,512,4096]{2,0,1:T(2,128)(2,1)} %get-tuple-element.322, s32[1024]{0:T(1024)S(1)} %pad_clamp_fusion.3), kind=kCustom, calls=%fused_computation.clone.1 | custom fusion | bytes 524352 | tf_op jit(solution)/shard_map/while/body/eval_jaxpr/jit(_take)/gather | solution.py:81
  341.6 1.1 fusion.146
  342.7 1.2 constant_dynamic-slice_fusion.4
  346.0 1.2 fusion.150
  347.3 3.2 fusion.151
  350.5 2.5 fusion.152
  353.0 2.6 fusion.153
  (125 shorter events, 26.3 us)
Async XLA Ops:
  7.2 138.3 %all-gather.3.cloned.1.call-start = ((), (), s32[]{:S(2)}) async-start(), calls=%async_computation | async-start | bytes 2162688 | tf_op jit(solution)/shard_map/all_gather | solution.py:106
  7.9 259.8 %all-gather.5.cloned.1.call-start = ((), (), s32[]{:S(2)}) async-start(), calls=%async_computation.1 | async-start | bytes 8650752 | tf_op jit(solution)/shard_map/all_gather | solution.py:123
  12.3 9.7 %copy-start.5 = (s32[64]{0:T(128)S(1)}, s32[64]{0:T(128)}, u32[]{:S(2)}) copy-start(s32[64]{0:T(128)} %param.14) | copy-start | bytes 772
  12.3 9.8 %copy-start.6 = (s32[64]{0:T(128)S(1)}, s32[64]{0:T(128)}, u32[]{:S(2)}) copy-start(s32[64]{0:T(128)} %param.13) | copy-start | bytes 772
  12.3 9.8 %copy-start.7 = (s32[64,1]{0,1:T(1,128)S(1)}, s32[64,1]{0,1:T(1,128)}, u32[]{:S(2)}) copy-start(s32[64,1]{0,1:T(1,128)} %param.12) | copy-start | bytes 772
  12.3 9.9 %copy-start.3 = (s32[64]{0:T(128)S(1)}, s32[64]{0:T(128)}, u32[]{:S(2)}) copy-start(s32[64]{0:T(128)} %param.15) | copy-start | bytes 772
  22.2 21.8 %copy-start.2 = (s32[16,15]{1,0:T(8,128)S(1)}, s32[16,15]{1,0:T(8,128)}, u32[]{:S(2)}) copy-start(s32[16,15]{1,0:T(8,128)} %param.11) | copy-start | bytes 2884
  22.2 120.6 %copy-start = (bf16[2,16,4096]{2,1,0:T(8,128)(2,1)S(1)}, bf16[2,16,4096]{2,1,0:T(8,128)(2,1)}, u32[]{:S(2)}) copy-start(bf16[2,16,4096]{2,1,0:T(8,128)(2,1)} %param.10) | copy-start | bytes 786436
  276.8 3.4 copy-start.1
  298.7 3.4 copy-start.1
  320.7 3.4 copy-start.1
  342.7 3.4 copy-start.1
  355.6 0.6 copy-start.4
Sparse Core Ops, SparseCore 0:
  11.1 75.5 all-gather.2
  89.8 101.7 all-gather.4
where the time goes:
time: 365 us; the launch traced here: 363 us
  matrix products  145 us (40%)
  blocking collectives  105 us (29%)
  other arithmetic  49.6 us (14%)
  local copies, waits for them, and re-layouts  47.9 us (13%)
  between operations  14.2 us (4%)
    all_gather x1, blocking collectives, body(): lax.all_gather(bounds, 'tmpl', axis=0, tiled=True)  98.2 us
    dot_general x1, matrix products, body(): jnp.dot(prod_im, sin_full, preferred_element_type=jnp.float32)  27.9 us
    dot_general x1, matrix products, body(): jnp.dot(prod_re, cos_full, preferred_element_type=jnp.float32)  27 us
    dot_general x1, matrix products, body(): jnp.dot(prod_re, sin_full, preferred_element_type=jnp.float32)  26.6 us
    dot_general x1, matrix products, body(): jnp.dot(prod_im, cos_full, preferred_element_type=jnp.float32)  25.9 us
    convert_element_type x1, other arithmetic, wave_table(): jnp.sin(angles).astype(jnp.bfloat16)  19.7 us
    gather x4, local copies, waits for them, and re-layouts, one_group(): jnp.take(bank, group_ids, axis=1)  17.8 us
    mul x4, matrix products, chi_square(): diff_im = corr_im - weight * whole_im  12.9 us
  transfers between devices with their start and end apart: 2, of which 0 were waited for; matrix products, arithmetic and copies ran while one was open for 43% of the time, Pallas kernels for 0%

commit v1 on v0

v1 whole, which is shorter than its diff:
```python
import math

import jax
import jax.numpy as jnp
import numpy as np
from jax import lax
from jax.experimental import pallas as pl
from jax.experimental.pallas import tpu as pltpu
from jax.sharding import PartitionSpec as P

F = 4096
NT = 16
NBINS = 16
EPSILON = 1e-06
BF = jnp.bfloat16
F32 = jnp.float32
I32 = jnp.int32
MESH = pl.DeviceIdType.MESH
ROWS_A = 144
ROWS = 272


def tables():
    step = 2.0 * math.pi / 4096.0
    phi = np.arange(4096, dtype=np.float64) - 2048.0
    half = np.arange(128, dtype=np.float64) + 0.5
    ang = step * phi[:, None] * half[None, :]
    main = np.concatenate([np.cos(ang), np.sin(ang)], 1)
    turn = (step * 127.5 * phi).reshape(32, 128)
    rot = np.stack([np.cos(turn), np.sin(turn)])
    near = step * np.arange(128.0)[:, None] * half[None, :]
    w0 = np.concatenate(
        [
            np.concatenate([np.cos(near), np.sin(near)], 1),
            np.concatenate([-np.sin(near), np.cos(near)], 1),
        ],
        0,
    )
    far = step * (128.0 * np.arange(32.0) - 2048.0)[:, None] * half[None, :]
    far = np.stack([np.cos(far), np.sin(far)])
    return (
        jnp.asarray(main, F32).astype(BF),
        jnp.asarray(rot, F32),
        jnp.asarray(w0, F32).astype(BF),
        jnp.asarray(far, F32).astype(BF),
    )


def iota(shape, dim):
    return lax.broadcasted_iota(I32, shape, dim)


def gather_kernel(block_ref, out_ref, send_sem, recv_sem, own_sem):
    me = lax.axis_index("tmpl")
    seg = lax.axis_index("seg")
    z, x, y = me // 16, (me // 4) % 4, me % 4

    def dev(zz, xx, yy):
        return zz * 16 + ((xx + 4) % 4) * 4 + (yy + 4) % 4

    peers = [dev(1 - z, x, y), dev(z, x + 1, y), dev(z, x - 1, y), dev(z, x, y + 1), dev(z, x, y - 1)]
    barrier = pltpu.get_barrier_semaphore()
    for peer in peers:
        pl.semaphore_signal(barrier, inc=1, device_id=(peer, seg), device_id_type=MESH)
    pl.semaphore_wait(barrier, 5)

    cuts = ((0, ROWS_A), (ROWS_A, ROWS - ROWS_A))
    started = [0, 0]
    copies = []

    def part(ref, half):
        return ref.at[pl.ds(cuts[half][0], cuts[half][1])]

    def send(half, source, peer, own=False):
        src = block_ref if own else out_ref.at[source]
        copy = pltpu.make_async_remote_copy(
            src_ref=part(src, half),
            dst_ref=part(out_ref.at[source], half),
            send_sem=send_sem.at[half, started[half]],
            recv_sem=recv_sem.at[half, source],
            device_id=(peer, seg),
            device_id_type=MESH,
        )
        started[half] += 1
        copy.start()
        copies.append(copy)

    def arrived(half, source):
        pltpu.make_async_remote_copy(
            src_ref=part(out_ref.at[source], half),
            dst_ref=part(out_ref.at[source], half),
            send_sem=send_sem.at[half, 0],
            recv_sem=recv_sem.at[half, source],
            device_id=(peers[0], seg),
            device_id_type=MESH,
        ).wait_recv()

    own = pltpu.make_async_copy(block_ref, out_ref.at[me], own_sem)
    own.start()

    def near(half, zz, step):
        return dev(zz, x + step, y) if half == 0 else dev(zz, x, y + step)

    def far(half, step):
        return dev(z, x, y + step) if half == 0 else dev(z, x + step, y)

    def fan(half, source, own=False):
        for step in (1, -1):
            send(half, source, far(half, step), own)

    for half in (0, 1):
        send(half, me, peers[0], True)
        for step in (1, -1):
            send(half, me, near(half, z, step), True)
    for half in (0, 1):
        fan(half, me, True)
    mate = peers[0]
    for half in (0, 1):
        arrived(half, mate)
        for step in (1, -1):
            send(half, mate, near(half, z, step))
        fan(half, mate)
    for same in (True, False):
        for step in (1, -1):
            for half in (0, 1):
                zz = z if same else 1 - z
                source = near(half, zz, step)
                arrived(half, source)
                if (same and step == 1) or (not same and step == -1):
                    send(half, source, near(half, z, -step))
                fan(half, source)
    for same in (True, False):
        for half in (0, 1):
            source = near(half, z if same else 1 - z, 2)
            arrived(half, source)
            fan(half, source)
    order = [(True, 0), (False, 0), (True, 1), (True, -1), (False, 1), (False, -1), (True, 2), (False, 2)]

    def cross(half, same, one, two):
        zz = z if same else 1 - z
        return dev(zz, x + one, y + two) if half == 0 else dev(zz, x + two, y + one)

    for n, (same, one) in enumerate(order):
        for two in (1, -1):
            for half in (0, 1):
                source = cross(half, same, one, two)
                arrived(half, source)
                if two == (1 if n % 2 == 0 else -1):
                    send(half, source, far(half, -two))
    for same, one in order:
        for half in (0, 1):
            arrived(half, cross(half, same, one, 2))
    own.wait()
    for copy in copies:
        copy.wait_send()


def gather(block):
    return pl.pallas_call(
        gather_kernel,
        out_shape=jax.ShapeDtypeStruct((32, ROWS, 128), BF),
        in_specs=[pl.BlockSpec(memory_space=pl.ANY)],
        out_specs=pl.BlockSpec(memory_space=pl.ANY),
        scratch_shapes=[
            pltpu.SemaphoreType.DMA((2, 31)),
            pltpu.SemaphoreType.DMA((2, 32)),
            pltpu.SemaphoreType.DMA,
        ],
        compiler_params=pltpu.CompilerParams(collective_id=0, has_side_effects=True),
        name="gather",
    )(block)


def prepare(tm_ref, bounds_ref, tmf, itp, masks, pick, weight):
    lane = iota((16, 128), 1)
    sub = iota((16, 128), 0)
    quarter, chunk = lane // 32, lane % 32
    cls = sub % 3
    nat = iota((32, 128), 0) * 128 + iota((32, 128), 1)
    freq = iota((16, F), 1)
    h0 = tm_ref[0].astype(F32)
    h1 = tm_ref[1].astype(F32)
    tmf[0] = h0
    tmf[1] = h1
    energy = h0 * h0 + h1 * h1
    rows16 = iota((16, 1), 0)

    def column(l):
        col = jnp.zeros((16, 1), I32)
        for m in range(NT):
            col = jnp.where(rows16 == m, bounds_ref[m, l], col)
        return col

    edges = [jnp.zeros((16, 1), I32)] + [column(l) for l in range(15)] + [jnp.full((16, 1), F, I32)]
    total = jnp.zeros((16, 1), F32)
    powers = jnp.zeros((16, 128), F32)
    for l in range(NBINS):
        inside = (freq >= edges[l]) & (freq < edges[l + 1])
        band = jnp.sum(jnp.where(inside, energy, 0.0), axis=1, keepdims=True) + EPSILON
        total = total + band
        powers = jnp.where(lane == l, band, powers)
    inverse = jnp.broadcast_to(1.0 / total, (16, 128))
    itp[...] = inverse
    for m in range(NT):
        low = jnp.zeros((16, 128), I32)
        high = jnp.full((16, 128), F, I32)
        for l in range(15):
            low = jnp.where(sub == l + 1, bounds_ref[m, l], low)
            high = jnp.where(sub == l, bounds_ref[m, l], high)
        touch = (cls == quarter) & (low < 128 * chunk + 128) & (high > 128 * chunk)
        whole = jnp.where((sub == 0) & (lane < 96), 1.0, 0.0)
        pick[m] = jnp.concatenate([jnp.where(touch, 1.0, 0.0), whole], 0)[:, :96].astype(BF)
        own = jnp.where(sub == lane, jnp.broadcast_to(powers[m : m + 1], (16, 128)), 0.0)
        own = jnp.sum(own, axis=1, keepdims=True)
        first = jnp.broadcast_to(1.0 / own, (16, 128))
        second = jnp.where(sub == 0, -jnp.broadcast_to(inverse[m : m + 1], (16, 128)), 0.0)
        weight[m] = jnp.concatenate([first, second], 0) * (1.0 / (2.0 * (NBINS - 1)))
        index = jnp.zeros((32, 128), I32)
        for l in range(15):
            index = index + jnp.where(nat >= bounds_ref[m, l], 1, 0)
        index = index - 3 * ((index * 11) >> 5)
        for q in range(3):
            masks[m, q] = jnp.where(index == q, 1.0, 0.0).astype(BF)


def spread(g_ref, rot_ref, turned, nat, sre, sim, group):
    rc, rs = rot_ref[0], rot_ref[1]
    for q in range(4):
        for k in range(8):
            a = group * 8 + k
            re = g_ref[a, pl.ds(32 * q, 32), :].astype(F32)
            im = g_ref[a, pl.ds(ROWS_A + 32 * q, 32), :].astype(F32)
            tr = re * rc - im * rs
            ti = re * rs + im * rc
            turned[a, q] = tr.astype(BF)
            turned[a, 4 + q] = ti.astype(BF)
            nat[0, q, pl.ds(k * 32, 32), :] = tr
            nat[1, q, pl.ds(k * 32, 32), :] = ti
    for q in range(4):
        for c in range(32):
            sre[group, pl.ds(8 * q, 8), pl.ds(c * 128, 128)] = nat[0, q, pl.ds(c, 8, stride=32), :]
            sim[group, pl.ds(8 * q, 8), pl.ds(c * 128, 128)] = nat[1, q, pl.ds(c, 8, stride=32), :]


def filters(table_ref, tmf, itp, sre, sim, lhs, snr_ref, peak, group, first):
    for n in range(4):
        for k in range(F // 256):
            cut = pl.ds(k * 256, 256)
            h0 = tmf[0, pl.ds(first + n, 1), cut]
            h1 = tmf[1, pl.ds(first + n, 1), cut]
            re = sre[group, :, cut]
            im = sim[group, :, cut]
            lhs[pl.ds(64 * n, 32), cut] = (re * h0 + im * h1).astype(BF)
            lhs[pl.ds(64 * n + 32, 32), cut] = (im * h0 - re * h1).astype(BF)
    acc = jnp.dot(lhs[...], table_ref[...], preferred_element_type=F32)
    back = 127 - iota((16, 128), 1)
    for n in range(4):
        a = acc[64 * n : 64 * n + 32, :128]
        d = acc[64 * n : 64 * n + 32, 128:]
        c = acc[64 * n + 32 : 64 * n + 64, :128]
        b = acc[64 * n + 32 : 64 * n + 64, 128:]
        plus = (a - b) * (a - b) + (c + d) * (c + d)
        minus = (a + b) * (a + b) + (c - d) * (c - d)
        scale = itp[pl.ds(first + n, 1), :]
        plus = (plus[:16] + plus[16:]) * scale
        minus = (minus[:16] + minus[16:]) * scale
        top = jnp.maximum(plus, minus)
        top = jnp.maximum(top[:8], top[8:])
        peak[first + n] = jnp.maximum(peak[first + n], top)
        minus = jnp.take_along_axis(minus, back, axis=1)
        for r in range(2):
            snr_ref[first + n, pl.ds(group * 32 + r, 8, stride=4), :] = minus[8 * r : 8 * r + 8]
            snr_ref[first + n, pl.ds(group * 32 + 2 + r, 8, stride=4), :] = plus[8 * r : 8 * r + 8]


def veto(w0_ref, far_ref, tn_ref, meta, turned, masks, pick, weight, chi_ref, a):
    fc, fs = far_ref[0], far_ref[1]
    lane = iota((1, 128), 1)
    rows = []
    at = []
    for k in range(4):
        m, r, blk = meta[a, k], meta[a, 4 + k], meta[a, 8 + k]
        at.append((m, blk))
        h0, h1 = tn_ref[0, m], tn_ref[1, m]
        sign = (2 * blk - 1).astype(F32).astype(BF)
        for d in range(2):
            re = turned[a, 2 * d + r]
            im = turned[a, 4 + 2 * d + r]
            xr = re * h0 + im * h1
            xi = (im * h0 - re * h1) * sign
            for q in range(3):
                mask = masks[m, q]
                rows.append(jnp.concatenate([xr * mask, xi * mask], 1))
    part = jnp.dot(jnp.concatenate(rows, 0), w0_ref[...], preferred_element_type=F32).astype(BF)
    for k in range(4):
        m, blk = at[k]
        s = jnp.zeros((32, 128), F32)
        for d in range(2):
            base = (2 * k + d) * 96
            turns = []
            for q in range(3):
                ur = part[base + 32 * q : base + 32 * q + 32, :128]
                ui = part[base + 32 * q : base + 32 * q + 32, 128:]
                turns.append(jnp.concatenate([ur * fc - ui * fs, ur * fs + ui * fc], 1))
            bands = jnp.dot(pick[m], jnp.concatenate(turns, 0), preferred_element_type=F32)
            s = s + bands[:, :128] * bands[:, :128] + bands[:, 128:] * bands[:, 128:]
        line = jnp.sum(s * weight[m], axis=0, keepdims=True)
        index = jnp.where(blk == 1, lane, 127 - lane)
        line = jnp.take_along_axis(
            jnp.broadcast_to(line, (8, 128)), jnp.broadcast_to(index, (8, 128)), axis=1
        )
        chi_ref[a, pl.ds(k, 1), :] = line[0:1]


def requests(g_ref, wanted):
    shard = lax.axis_index("tmpl").astype(F32)
    rows = [g_ref[:, 128 + v, :].astype(F32) for v in range(4)]
    lane = iota((32, 128), 1)
    hit = (rows[0] == shard) & (lane < 64)
    before = jnp.where(iota((128, 128), 0) < iota((128, 128), 1), 1.0, 0.0).astype(BF)
    rank = jnp.dot(jnp.where(hit, 1.0, 0.0).astype(BF), before, preferred_element_type=F32)
    table = jnp.zeros((32, 128), F32)
    for v in range(3):
        for k in range(4):
            value = jnp.sum(jnp.where(hit & (rank == float(k)), rows[v + 1], 0.0), axis=1, keepdims=True)
            table = jnp.where(lane == 4 * v + k, value, table)
    wanted[...] = table.astype(I32)


def compute_kernel(
    g_ref, tm_ref, tn_ref, bounds_ref, table_ref, rot_ref, w0_ref, far_ref,
    snr_ref, peak_ref, chi_ref,
    tmf, itp, masks, pick, weight, turned, nat, sre, sim, lhs, peak, wanted, meta, sem,
):
    requests(g_ref, wanted)
    copy = pltpu.make_async_copy(wanted, meta, sem)
    copy.start()
    prepare(tm_ref, bounds_ref, tmf, itp, masks, pick, weight)
    chi_ref[...] = jnp.zeros_like(chi_ref)
    peak[...] = jnp.zeros_like(peak)
    copy.wait()

    @pl.loop(0, 4)
    def _(group):
        spread(g_ref, rot_ref, turned, nat, sre, sim, group)

    @pl.loop(0, 16)
    def _(step):
        filters(table_ref, tmf, itp, sre, sim, lhs, snr_ref, peak, step // 4, (step % 4) * 4)

    @pl.loop(0, 32)
    def _(a):
        veto(w0_ref, far_ref, tn_ref, meta, turned, masks, pick, weight, chi_ref, a)

    for m in range(NT):
        peak_ref[pl.ds(m, 1), :] = jnp.max(peak[m], axis=0, keepdims=True)


def compute(gathered, templates, bounds, wave, rot, w0, far):
    vmem = pl.BlockSpec(memory_space=pltpu.VMEM)
    smem = pl.BlockSpec(memory_space=pltpu.SMEM)
    return pl.pallas_call(
        compute_kernel,
        out_shape=(
            jax.ShapeDtypeStruct((NT, 128, 128), F32),
            jax.ShapeDtypeStruct((NT, 128), F32),
            jax.ShapeDtypeStruct((32, 8, 128), F32),
        ),
        in_specs=[vmem, vmem, vmem, smem, vmem, vmem, vmem, vmem],
        out_specs=(vmem, vmem, vmem),
        scratch_shapes=[
            pltpu.VMEM((2, NT, F), F32),
            pltpu.VMEM((NT, 128), F32),
            pltpu.VMEM((NT, 3, 32, 128), BF),
            pltpu.VMEM((NT, 32, 96), BF),
            pltpu.VMEM((NT, 32, 128), F32),
            pltpu.VMEM((32, 8, 32, 128), BF),
            pltpu.VMEM((2, 4, 256, 128), F32),
            pltpu.VMEM((4, 32, F), F32),
            pltpu.VMEM((4, 32, F), F32),
            pltpu.VMEM((256, F), BF),
            pltpu.VMEM((NT, 8, 128), F32),
            pltpu.VMEM((32, 128), I32),
            pltpu.SMEM((32, 128), I32),
            pltpu.SemaphoreType.DMA,
        ],
        compiler_params=pltpu.CompilerParams(vmem_limit_bytes=48 * 1024 * 1024),
        name="compute",
    )(gathered, templates, templates.reshape(2, NT, 32, 128), bounds, wave, rot, w0, far)


def home_kernel(chi_ref, peak_ref, owner_ref, out_ref, loud_ref, slots, peaks, send_sem, recv_sem, pair_send, pair_recv):
    me = lax.axis_index("tmpl")
    seg = lax.axis_index("seg")
    barrier = pltpu.get_barrier_semaphore()
    for j in range(1, 32):
        pl.semaphore_signal(barrier, inc=1, device_id=((me + j) % 32, seg), device_id_type=MESH)
    for j in range(1, 4):
        pl.semaphore_signal(barrier, inc=1, device_id=(me, (seg + j) % 4), device_id_type=MESH)
    pl.semaphore_wait(barrier, 34)
    copies = []
    for j in range(1, 32):
        peer = (me + j) % 32
        copies.append(
            pltpu.make_async_remote_copy(
                src_ref=chi_ref.at[peer],
                dst_ref=slots.at[me],
                send_sem=send_sem.at[j],
                recv_sem=recv_sem.at[j],
                device_id=(peer, seg),
                device_id_type=MESH,
            )
        )
    for j in range(1, 4):
        copies.append(
            pltpu.make_async_remote_copy(
                src_ref=peak_ref,
                dst_ref=peaks.at[j],
                send_sem=pair_send.at[j],
                recv_sem=pair_recv.at[j],
                device_id=(me, (seg + j) % 4),
                device_id_type=MESH,
            )
        )
    for copy in copies:
        copy.start()
    slots[pl.ds(me, 1)] = chi_ref[pl.ds(me, 1)]
    owner = owner_ref[...]
    i, j = iota((64, 64), 0), iota((64, 64), 1)
    across = jnp.sum(jnp.where(i == j, owner, 0), axis=0, keepdims=True)
    rank = jnp.sum(jnp.where((j < i) & (across == owner), 1, 0), axis=1, keepdims=True)
    choose = jnp.where(iota((64, 256), 1) == owner * 8 + rank, 1.0, 0.0)
    for copy in copies:
        copy.wait()
    out_ref[...] = jnp.dot(
        choose,
        slots[...].reshape(256, 128),
        preferred_element_type=F32,
        precision=lax.Precision.HIGHEST,
    )
    top = jnp.maximum(jnp.maximum(peak_ref[...], peaks[1]), jnp.maximum(peaks[2], peaks[3]))
    top = jnp.max(top, axis=1, keepdims=True)
    loud_ref[...] = jnp.max(jnp.where(iota((NT, 128), 0) == iota((NT, 128), 1), top, 0.0), axis=0, keepdims=True)


def home(chi, peak, owner):
    vmem = pl.BlockSpec(memory_space=pltpu.VMEM)
    return pl.pallas_call(
        home_kernel,
        out_shape=(jax.ShapeDtypeStruct((64, 128), F32), jax.ShapeDtypeStruct((1, 128), F32)),
        in_specs=[vmem] * 3,
        out_specs=(vmem, vmem),
        scratch_shapes=[
            pltpu.VMEM((32, 8, 128), F32),
            pltpu.VMEM((4, NT, 128), F32),
            pltpu.SemaphoreType.DMA((32,)),
            pltpu.SemaphoreType.DMA((32,)),
            pltpu.SemaphoreType.DMA((4,)),
            pltpu.SemaphoreType.DMA((4,)),
        ],
        compiler_params=pltpu.CompilerParams(collective_id=1, has_side_effects=True),
        name="home",
    )(chi, peak, owner)


def body(
    spectra, templates, bounds, trigger_owner, trigger_template, trigger_segment, trigger_block
):
    wave, rot, w0, far = tables()
    parts = spectra.reshape(2, 128, 128)
    listed = jnp.stack([trigger_owner[:, 0], trigger_template, trigger_segment, trigger_block])
    listed = jnp.pad(listed.astype(BF), ((0, 12), (0, 64)))
    block = jnp.concatenate([parts[0], listed, parts[1]], axis=0)
    gathered = gather(block)
    snr, peak, chi = compute(gathered, templates, bounds, wave, rot, w0, far)
    chisq, loud = home(chi, peak, trigger_owner)
    snr = snr.reshape(NT, 32, 2, 2, 128).transpose(0, 1, 3, 2, 4).reshape(NT, 32, 2, 256)
    return snr, loud[0, :NT], chisq


def solution(mesh):
    in_specs = (
        P(None, None, "tmpl", "seg", None),
        P(None, "tmpl", None),
        P("tmpl", None),
        P(("tmpl", "seg"), None),
        P(("tmpl", "seg")),
        P(("tmpl", "seg")),
        P(("tmpl", "seg")),
    )
    out_specs = (P("tmpl", None, "seg", None), P("tmpl"), P(("tmpl", "seg"), None))
    return jax.shard_map(body, mesh=mesh, in_specs=in_specs, out_specs=out_specs, check_vma=False)
```

time: 365 us -> 90.6 us (0.25)
  matrix products: 145 us -> 0 us
  blocking collectives: 105 us -> 0 us
  Pallas kernels: 0 us -> 79.6 us
  other arithmetic: 49.6 us -> 2.81 us
  local copies, waits for them, and re-layouts: 47.9 us -> 7.03 us
  between operations: 14.2 us -> 0.79 us
    dot_general x12 -> x0, matrix products: 122 us -> none  [the longest x1 27.9 us: body(): jnp.dot(prod_im, sin_full, preferred_element_type=jnp.float32)]
    all_gather x1 -> x0, blocking collectives: 98.2 us -> none  [body(): lax.all_gather(bounds, 'tmpl', axis=0, tiled=True)]
    pallas_call x0 -> x3, Pallas kernels: none -> 79.6 us  [the longest x1 37.9 us: compute(): pl.pallas_call(compute_kernel, out_shape=(jax.ShapeDtypeStruct((NT, 128,...]
    gather x10 -> x0, local copies, waits for them, and re-layouts: 29.7 us -> none  [the longest x4 17.8 us: one_group(): jnp.take(bank, group_ids, axis=1)]
    convert_element_type x14 -> x0, other arithmetic: 28.2 us -> none  [the longest x1 19.7 us: wave_table(): jnp.sin(angles).astype(jnp.bfloat16)]
    mul x8 -> x0, matrix products: 23.1 us -> none  [the longest x4 12.9 us: chi_square(): diff_im = corr_im - weight * whole_im]
    pmax x1 -> x0, blocking collectives: 6.39 us -> none  [body(): loudest = lax.pmax(jnp.max(network_snr, axis=(1, 2, 3)), 'seg')]
    reduce_sum x11 -> x0, other arithmetic: 6.18 us -> none  [the longest x5 3.3 us: band_split(): jnp.sum(jnp.where(bin_mask, energy[:, None, :], 0.0), axis=2) + EPSILON]
  transfers between devices with their start and end apart: 2 -> 0, of which waited for: 0 -> 0; matrix products, arithmetic and copies ran while one was open for 43% -> 0% of each run, Pallas kernels for 0% -> 0%
where the time goes in v1:
time: 90.6 us; the launch traced here: 90.2 us
  Pallas kernels  79.6 us (88%)
  local copies, waits for them, and re-layouts  7.03 us (8%)
  other arithmetic  2.81 us (3%)
    pallas_call x1, Pallas kernels, compute(): pl.pallas_call(compute_kernel, out_shape=(jax.ShapeDtypeStruct((NT, 128,...  37.9 us
    pallas_call x1, Pallas kernels, gather(): pl.pallas_call(gather_kernel, out_shape=jax.ShapeDtypeStruct((32, ROWS, 1...  28.1 us
    pallas_call x1, Pallas kernels, home(): pl.pallas_call(home_kernel, out_shape=(jax.ShapeDtypeStruct((64, 128), F3...  13.7 us
    unnamed x23, local copies, waits for them, and re-layouts  5.02 us
    another operation x4, other arithmetic, body(): jnp.stack([trigger_owner[:, 0], trigger_template, trigger_segment, trigge...  2.18 us

profile of v1, /device:TPU:0, one launch (start us, length us, event | category | flops | bytes accessed | tf_op | source)
XLA Modules:
  0.0 90.2 jit_solution(13475751790436892883)
XLA Ops:
  0.6 0.0 copy-start.5
  0.6 0.0 copy-start.1
  0.7 0.0 copy-start.3
  0.7 0.0 copy-start.6
  0.7 0.0 copy-start.2
  0.7 0.0 copy-start.7
  0.7 0.8 convert_bitcast_fusion
  1.5 0.7 convert_bitcast_fusion.2
  2.2 0.7 convert_bitcast_fusion.3
  2.9 0.8 fusion.12
  3.8 0.6 pad_maximum_fusion.block_ref
  4.4 28.1 %gather.1.g_ref = bf16[32,272,128]{2,1,0:T(8,128)(2,1)} custom-call(bf16[272,128]{1,0:T(8,128)(2,1)} %pad_maximum_fusion.block_ref), custom_call_target="tpu_custom_call" | custom-call | tf_op jit(solution)/shard_map/gather/pallas_call | solution.py:159
  32.5 0.0 copy-done.2
  32.5 0.0 copy-done.5
  32.5 0.0 copy-done.1
  32.6 0.0 copy-done.3
  32.6 0.0 copy-done.6
  32.6 0.0 copy-done.7
  32.6 0.0 copy-start
  32.6 1.6 %copy-done = bf16[32,272,128]{2,1,0:T(8,128)(2,1)S(1)} copy-done((bf16[32,272,128]{2,1,0:T(8,128)(2,1)S(1)}, bf16[32,272,128]{2,1,0:T(8,128)(2,1)}, u32[]{:S(2)}) %copy-start) | copy-done | bytes 2228248
  34.2 0.0 copy-start.9
  34.2 37.9 %compute.1 = (f32[16,128,128]{2,1,0:T(8,128)}, f32[16,128]{1,0:T(8,128)S(1)}, f32[32,8,128]{2,1,0:T(8,128)S(1)}) custom-call(bf16[32,272,128]{2,1,0:T(8,128)(2,1)S(1)} %copy-done, bf16[2,16,4096]{2,1,0:T(8,128)(2,1)S(1)} %copy-done.2, bf16[2,16,32,128]{3,2,1,0:T(8,128)(2,1)S(1)} %bitcast.20, s32[16,15]{1,0:T(8,128)S(1)} %copy-done.7, ...), custom_call_target="tpu_custom_call" | custom-call | tf_op jit(solution)/shard_map/compute/pallas_call | solution.py:362
  72.1 0.0 copy-start.4
  72.1 0.6 copy-done.4
  72.8 0.0 copy-start.8
  72.8 0.6 copy-done.8
  73.4 0.0 copy-done.9
  73.4 0.7 copy.15.owner_ref
  74.1 13.7 %home.1 = (f32[64,128]{1,0:T(8,128)}, f32[1,128]{1,0:T(1,128)}) custom-call(f32[32,8,128]{2,1,0:T(8,128)} %copy-done.4, f32[16,128]{1,0:T(8,128)} %copy-done.8, s32[64,1]{1,0:T(8,128)} %copy.15.owner_ref), custom_call_target="tpu_custom_call" | custom-call | tf_op jit(solution)/shard_map/home/pallas_call | solution.py:448
  87.8 1.1 %slice_bitcast_fusion = f32[16]{0:T(128)} fusion(f32[1,128]{1,0:T(1,128)} %get-tuple-element.11), kind=kLoop, calls=%fused_computation.15 | loop fusion | bytes 128 | tf_op jit(solution)/shard_map/squeeze | solution.py:478
  88.9 1.4 %copy.18 = f32[64,128]{1,0:T(8,128)} copy(f32[64,128]{1,0:T(8,128)} %get-tuple-element.22) | data formatting | bytes 65536
  (4 shorter events, 0.1 us)
Async XLA Ops:
  0.6 31.9 %copy-start.5 = (f32[2,32,128]{2,1,0:T(8,128)S(1)}, f32[2,32,128]{2,1,0:T(8,128)}, u32[]{:S(2)}) copy-start(f32[2,32,128]{2,1,0:T(8,128)} %constant.12.clone.rot_ref) | copy-start | bytes 98308
  0.6 31.9 %copy-start.1 = (bf16[4096,256]{1,0:T(8,128)(2,1)S(1)}, bf16[4096,256]{1,0:T(8,128)(2,1)}, u32[]{:S(2)}) copy-start(bf16[4096,256]{1,0:T(8,128)(2,1)} %constant.24.table_ref) | copy-start | bytes 6291460
  0.7 31.9 %copy-start.3 = (bf16[256,256]{1,0:T(8,128)(2,1)S(1)}, bf16[256,256]{1,0:T(8,128)(2,1)}, u32[]{:S(2)}) copy-start(bf16[256,256]{1,0:T(8,128)(2,1)} %constant.25.w0_ref) | copy-start | bytes 393220
  0.7 31.9 %copy-start.6 = (bf16[2,32,128]{2,1,0:T(8,128)(2,1)S(1)}, bf16[2,32,128]{2,1,0:T(8,128)(2,1)}, u32[]{:S(2)}) copy-start(bf16[2,32,128]{2,1,0:T(8,128)(2,1)} %constant.26.far_ref) | copy-start | bytes 49156
  0.7 31.8 %copy-start.2 = (bf16[2,16,4096]{2,1,0:T(8,128)(2,1)S(1)}, bf16[2,16,4096]{2,1,0:T(8,128)(2,1)}, u32[]{:S(2)}) copy-start(bf16[2,16,4096]{2,1,0:T(8,128)(2,1)} %tm_ref.1) | copy-start | bytes 786436
  0.7 31.9 %copy-start.7 = (s32[16,15]{1,0:T(8,128)S(1)}, s32[16,15]{1,0:T(8,128)}, u32[]{:S(2)}) copy-start(s32[16,15]{1,0:T(8,128)} %bounds_ref.1) | copy-start | bytes 2884
  32.6 1.6 %copy-start = (bf16[32,272,128]{2,1,0:T(8,128)(2,1)S(1)}, bf16[32,272,128]{2,1,0:T(8,128)(2,1)}, u32[]{:S(2)}) copy-start(bf16[32,272,128]{2,1,0:T(8,128)(2,1)} %gather.1.g_ref) | copy-start | bytes 6684676
  34.2 39.1 %copy-start.9 = (s32[64,1]{0,1:T(1,128)S(1)}, s32[64,1]{0,1:T(1,128)}, u32[]{:S(2)}) copy-start(s32[64,1]{0,1:T(1,128)} %param.14) | copy-start | bytes 772
  72.1 0.7 copy-start.4
  72.8 0.6 copy-start.8

commit v2 on v0

v2 whole, which is shorter than its diff:
```python
import math

import jax
import jax.numpy as jnp
import numpy as np
from jax import lax
from jax.experimental import pallas as pl
from jax.experimental.pallas import tpu as pltpu
from jax.sharding import PartitionSpec as P

F = 4096
NT = 16
NBINS = 16
EPSILON = 1e-06
BF = jnp.bfloat16
F32 = jnp.float32
I32 = jnp.int32
MESH = pl.DeviceIdType.MESH
ROWS_A = 144
ROWS = 272


def tables():
    step = 2.0 * math.pi / 4096.0
    phi = np.arange(4096, dtype=np.float64) - 2048.0
    half = np.arange(128, dtype=np.float64) + 0.5
    ang = step * phi[:, None] * half[None, :]
    main = np.concatenate([np.cos(ang), np.sin(ang)], 1)
    turn = (step * 127.5 * phi).reshape(32, 128)
    rot = np.stack([np.cos(turn), np.sin(turn)])
    near = step * np.arange(128.0)[:, None] * half[None, :]
    w0 = np.concatenate(
        [
            np.concatenate([np.cos(near), np.sin(near)], 1),
            np.concatenate([-np.sin(near), np.cos(near)], 1),
        ],
        0,
    )
    far = step * (128.0 * np.arange(32.0) - 2048.0)[:, None] * half[None, :]
    far = np.stack([np.cos(far), np.sin(far)])
    return (
        jnp.asarray(main, F32).astype(BF),
        jnp.asarray(rot, F32),
        jnp.asarray(w0, F32).astype(BF),
        jnp.asarray(far, F32).astype(BF),
    )


def iota(shape, dim):
    return lax.broadcasted_iota(I32, shape, dim)


def ring(zz, xx, yy):
    return zz * 16 + xx % 4 * 4 + yy % 4


class Torus:
    def __init__(self, held, full_sem, half_sem, recv_sem):
        self.me = lax.axis_index("tmpl")
        self.seg = lax.axis_index("seg")
        self.z, self.x, self.y = self.me // 16, self.me // 4 % 4, self.me % 4
        self.held, self.full_sem, self.half_sem, self.recv_sem = held, full_sem, half_sem, recv_sem

    def step(self, kind, near, far, here=False):
        plane = self.z if kind == 0 else 1 - self.z
        xx = self.x + near * (1 - plane) + far * plane
        yy = self.y + near * plane + far * (1 - plane)
        return ring(self.z if here else plane, xx, yy)

    def member(self, delta, k):
        plane, at = k // 4, k % 4
        first = at * 4 + (self.y + delta) % 4
        second = 16 + (self.x + delta) % 4 * 4 + at
        return (1 - plane) * first + plane * second

    def copy(self, source, peer, half, sem):
        if half is None:
            view, recv, send = self.held.at[source], self.recv_sem.at[0, source], self.full_sem.at[sem]
        else:
            cut = pl.ds(0, ROWS_A) if half == 0 else pl.ds(ROWS_A, ROWS - ROWS_A)
            view, recv, send = self.held.at[source, cut], self.recv_sem.at[half, source], self.half_sem.at[half, sem]
        return pltpu.make_async_remote_copy(
            src_ref=view, dst_ref=view, send_sem=send, recv_sem=recv, device_id=(peer, self.seg), device_id_type=MESH
        )

    def arrive(self, source, halves=False):
        peer = ring(1 - self.z, self.x, self.y)
        for half in (0, 1) if halves else (None,):
            self.copy(source, peer, half, 0).wait_recv()

    def fan(self, kind, near):
        source = self.step(kind, near, 0)
        for n, far in enumerate((1, 3)):
            self.copy(source, self.step(kind, 0, far, True), None, 5 + kind * 8 + near * 2 + n).start()

    def sides(self, kind):
        source = self.step(kind, 0, 0)
        for n, near in enumerate((1, 3)):
            self.copy(source, self.step(kind, near, 0, True), None, 1 + kind * 2 + n).start()

    def begin(self):
        mate = ring(1 - self.z, self.x, self.y)
        self.copy(self.me, mate, None, 0).start()
        self.sides(0)
        self.fan(0, 0)

    def first(self):
        self.arrive(self.step(1, 0, 0))
        self.sides(1)
        self.fan(1, 0)
        for near in (1, 3):
            for kind in (0, 1):
                source = self.step(kind, near, 0)
                self.arrive(source)
                self.copy(source, self.step(kind, 4 - near, 0, True), 1 if near == 1 else 0, kind).start()
                self.fan(kind, near)
        for kind in (0, 1):
            self.arrive(self.step(kind, 2, 0), True)
            self.fan(kind, 2)

    def onward(self, near):
        for kind in (0, 1):
            for far in (1, 3):
                source = self.step(kind, near, far)
                self.arrive(source)
                self.copy(source, self.step(kind, 0, 4 - far, True), 1 if far == 1 else 0, 2 + kind * 4 + near).start()

    def last(self):
        @pl.loop(0, 4)
        def _(near):
            for kind in (0, 1):
                self.arrive(self.step(kind, near, 2), True)

    def finish(self):
        peer = ring(1 - self.z, self.x, self.y)

        @pl.loop(0, 21)
        def _(n):
            self.copy(self.me, peer, None, n).wait_send()

        @pl.loop(0, 10)
        def _(n):
            for half in (0, 1):
                self.copy(self.me, peer, half, n).wait_send()


def lay_out(spec_ref, own_ref, tmpl_ref, seg_ref, blk_ref, tm_ref, held, tn, nat, listed, me):
    listed[...] = jnp.zeros_like(listed)
    for v, ref in enumerate((own_ref, tmpl_ref, seg_ref, blk_ref)):
        listed[pl.ds(v, 1), pl.ds(0, 64)] = ref[...].astype(F32)
    held[me, pl.ds(128, 16), :] = listed[...].astype(BF)
    for p in range(2):
        for d in range(2):
            value = spec_ref[p, d].astype(F32)
            for c in range(32):
                nat[p, d, pl.ds(c, 2, stride=32), :] = value[:, 128 * c : 128 * c + 128]
    for p in range(2):
        for d in range(2):
            held[me, pl.ds(p * ROWS_A + 64 * d, 64), :] = nat[p, d, pl.ds(0, 64), :].astype(BF)


def prepare(tm_ref, bounds_ref, tmf, tn, nat, itp, masks, pick, weight):
    lane = iota((16, 128), 1)
    sub = iota((16, 128), 0)
    quarter, chunk = lane // 32, lane % 32
    cls = sub % 3
    natural = iota((32, 128), 0) * 128 + iota((32, 128), 1)
    freq = iota((16, F), 1)
    h0 = tm_ref[0].astype(F32)
    h1 = tm_ref[1].astype(F32)
    tmf[0] = h0
    tmf[1] = h1
    for p in range(2):
        for h in range(2):
            for c in range(32):
                nat[p, h, pl.ds(c, 8, stride=32), :] = tmf[p, pl.ds(8 * h, 8), pl.ds(128 * c, 128)]
            for m in range(8):
                tn[p, 8 * h + m] = nat[p, h, pl.ds(32 * m, 32), :].astype(BF)
    energy = h0 * h0 + h1 * h1
    rows16 = iota((16, 1), 0)

    def column(l):
        col = jnp.zeros((16, 1), I32)
        for m in range(NT):
            col = jnp.where(rows16 == m, bounds_ref[m, l], col)
        return col

    edges = [jnp.zeros((16, 1), I32)] + [column(l) for l in range(15)] + [jnp.full((16, 1), F, I32)]
    total = jnp.zeros((16, 1), F32)
    powers = jnp.zeros((16, 128), F32)
    for l in range(NBINS):
        inside = (freq >= edges[l]) & (freq < edges[l + 1])
        band = jnp.sum(jnp.where(inside, energy, 0.0), axis=1, keepdims=True) + EPSILON
        total = total + band
        powers = jnp.where(lane == l, band, powers)
    inverse = jnp.broadcast_to(1.0 / total, (16, 128))
    itp[...] = inverse
    none = jnp.zeros((16, 96), F32)
    short = iota((16, 96), 0)
    sums = jnp.concatenate([jnp.where(short == 0, 1.0, none), jnp.where(short == 1, 1.0, none)], 1)
    for m in range(NT):
        low = jnp.zeros((16, 128), I32)
        high = jnp.full((16, 128), F, I32)
        index = jnp.zeros((32, 128), I32)
        for l in range(15):
            edge = bounds_ref[m, l]
            low = jnp.where(sub == l + 1, edge, low)
            high = jnp.where(sub == l, edge, high)
            index = index + jnp.where(natural >= edge, 1, 0)
        touch = (cls == quarter) & (low < 128 * chunk + 128) & (high > 128 * chunk)
        touch = jnp.where(touch, 1.0, 0.0)[:, :96]
        pick[m] = jnp.concatenate(
            [jnp.concatenate([touch, none], 1), jnp.concatenate([none, touch], 1), sums], 0
        ).astype(BF)
        own = jnp.where(sub == lane, jnp.broadcast_to(powers[m : m + 1], (16, 128)), 0.0)
        own = jnp.sum(own, axis=1, keepdims=True)
        bands = jnp.broadcast_to(1.0 / own, (16, 128))
        whole = jnp.where(sub < 2, -jnp.broadcast_to(inverse[m : m + 1], (16, 128)), 0.0)
        weight[m] = jnp.concatenate([bands, bands, whole], 0) * (1.0 / (2.0 * (NBINS - 1)))
        index = index - 3 * ((index * 11) >> 5)
        for q in range(3):
            masks[m, q] = jnp.where(index == q, 1.0, 0.0).astype(BF)


def spread(place, held, rot_ref, turned, nat, sre, sim, delta):
    rc, rs = rot_ref[0], rot_ref[1]

    @pl.loop(0, 8)
    def _(k):
        a = place.member(delta, k)
        for q in range(4):
            re = held[a, pl.ds(32 * q, 32), :].astype(F32)
            im = held[a, pl.ds(ROWS_A + 32 * q, 32), :].astype(F32)
            tr = re * rc - im * rs
            ti = re * rs + im * rc
            turned[k, q] = tr.astype(BF)
            turned[k, 4 + q] = ti.astype(BF)
            nat[0, q, pl.ds(k * 32, 32), :] = tr
            nat[1, q, pl.ds(k * 32, 32), :] = ti

    for q in range(4):
        for c in range(32):
            sre[pl.ds(8 * q, 8), pl.ds(c * 128, 128)] = nat[0, q, pl.ds(c, 8, stride=32), :]
            sim[pl.ds(8 * q, 8), pl.ds(c * 128, 128)] = nat[1, q, pl.ds(c, 8, stride=32), :]


def requests(place, held, wanted, meta, sem, delta):
    shard = place.me.astype(F32)
    tiles = [held[place.member(delta, k), pl.ds(128, 16), :].astype(F32) for k in range(8)]
    rows = [jnp.concatenate([t[v : v + 1] for t in tiles], 0) for v in range(4)]
    lane = iota((8, 128), 1)
    hit = (rows[0] == shard) & (lane < 64)
    before = jnp.where(iota((128, 128), 0) < iota((128, 128), 1), 1.0, 0.0).astype(BF)
    rank = jnp.dot(jnp.where(hit, 1.0, 0.0).astype(BF), before, preferred_element_type=F32)
    table = jnp.zeros((8, 128), F32)
    for v in range(3):
        for k in range(4):
            value = jnp.sum(jnp.where(hit & (rank == float(k)), rows[v + 1], 0.0), axis=1, keepdims=True)
            table = jnp.where(lane == 4 * v + k, value, table)
    wanted[...] = table.astype(I32)
    copy = pltpu.make_async_copy(wanted, meta, sem)
    copy.start()
    copy.wait()


def veto(w0_ref, far_ref, tn, meta, turned, masks, pick, weight, chi, slot, source):
    fc, fs = far_ref[0], far_ref[1]
    rows = []
    at = []
    for k in range(4):
        m = jnp.clip(meta[slot, k], 0, NT - 1)
        r = jnp.clip(meta[slot, 4 + k], 0, 1)
        blk = jnp.clip(meta[slot, 8 + k], 0, 1)
        at.append((m, blk))
        h0, h1 = tn[0, m], tn[1, m]
        sign = (2 * blk - 1).astype(F32).astype(BF)
        for d in range(2):
            re = turned[slot, 2 * d + r]
            im = turned[slot, 4 + 2 * d + r]
            xr = re * h0 + im * h1
            xi = (im * h0 - re * h1) * sign
            for q in range(3):
                mask = masks[m, q]
                rows.append(jnp.concatenate([xr * mask, xi * mask], 1))
    part = jnp.dot(jnp.concatenate(rows, 0), w0_ref[...], preferred_element_type=F32).astype(BF)
    lines = []
    for k in range(4):
        m, blk = at[k]
        turns = []
        for q in range(6):
            base = k * 192 + 32 * q
            ur = part[base : base + 32, :128]
            ui = part[base : base + 32, 128:]
            turns.append(jnp.concatenate([ur * fc - ui * fs, ur * fs + ui * fc], 1))
        bands = jnp.dot(pick[m], jnp.concatenate(turns, 0), preferred_element_type=F32)
        s = bands[:, :128] * bands[:, :128] + bands[:, 128:] * bands[:, 128:]
        lines.append((blk, jnp.sum(s * weight[m], axis=0, keepdims=True)))
    value = jnp.concatenate([line for _, line in lines] * 2, 0)
    back = jnp.take_along_axis(value, 127 - iota((8, 128), 1), axis=1)
    sub = iota((8, 128), 0) % 4
    late = jnp.zeros((8, 128), I32)
    for k in range(4):
        late = jnp.where(sub == k, lines[k][0], late)
    chi[source] = jnp.where(late == 1, value, back)


def filters(place, table_ref, tmf, itp, sre, sim, lhs, snr_ref, peak, delta, first):
    for n in range(4):
        for k in range(F // 256):
            cut = pl.ds(k * 256, 256)
            h0 = tmf[0, pl.ds(first + n, 1), cut]
            h1 = tmf[1, pl.ds(first + n, 1), cut]
            re = sre[:, cut]
            im = sim[:, cut]
            lhs[pl.ds(64 * n, 32), cut] = (re * h0 + im * h1).astype(BF)
            lhs[pl.ds(64 * n + 32, 32), cut] = (im * h0 - re * h1).astype(BF)
    acc = jnp.dot(lhs[...], table_ref[...], preferred_element_type=F32)
    back = 127 - iota((16, 128), 1)
    one = (place.y + delta) % 4 * 4
    two = 64 + (place.x + delta) % 4 * 16
    for n in range(4):
        a = acc[64 * n : 64 * n + 32, :128]
        d = acc[64 * n : 64 * n + 32, 128:]
        c = acc[64 * n + 32 : 64 * n + 64, :128]
        b = acc[64 * n + 32 : 64 * n + 64, 128:]
        plus = (a - b) * (a - b) + (c + d) * (c + d)
        minus = (a + b) * (a + b) + (c - d) * (c - d)
        scale = itp[pl.ds(first + n, 1), :]
        plus = (plus[:16] + plus[16:]) * scale
        minus = (minus[:16] + minus[16:]) * scale
        top = jnp.maximum(plus, minus)
        top = jnp.maximum(top[:8], top[8:])
        peak[first + n] = jnp.maximum(peak[first + n], top)
        minus = jnp.take_along_axis(minus, back, axis=1)
        for half, value in enumerate((minus, plus)):
            for r in range(2):
                to = 2 * half + r
                snr_ref[first + n, pl.ds(one + to, 4, stride=16), :] = value[8 * r : 8 * r + 4]
                for k in range(4):
                    line = value[8 * r + 4 + k : 8 * r + 5 + k]
                    snr_ref[first + n, pl.ds(two + to + 4 * k, 1), :] = line


def kernel(
    spec_ref, tm_ref, bounds_ref, own_ref, tmpl_ref, seg_ref, blk_ref, table_ref, rot_ref, w0_ref, far_ref,
    snr_ref, loud_ref, out_ref,
    held, listed, tmf, tn, itp, masks, pick, weight, turned, nat, sre, sim, lhs, peak, wanted, meta,
    chi, slots, tops, peaks,
    full_sem, half_sem, recv_sem, meta_sem, chi_send, chi_recv, pair_send, pair_recv,
):
    place = Torus(held, full_sem, half_sem, recv_sem)
    me, seg = place.me, place.seg
    barrier = pltpu.get_barrier_semaphore()

    @pl.loop(1, 32)
    def _(j):
        pl.semaphore_signal(barrier, inc=1, device_id=((me + j) % 32, seg), device_id_type=MESH)

    for j in range(1, 4):
        pl.semaphore_signal(barrier, inc=1, device_id=(me, (seg + j) % 4), device_id_type=MESH)
    lay_out(spec_ref, own_ref, tmpl_ref, seg_ref, blk_ref, tm_ref, held, tn, nat, listed, me)
    pl.semaphore_wait(barrier, 34)
    place.begin()
    prepare(tm_ref, bounds_ref, tmf, tn, nat, itp, masks, pick, weight)
    peak[...] = jnp.zeros_like(peak)
    place.first()

    def result(source):
        return pltpu.make_async_remote_copy(
            src_ref=chi.at[source],
            dst_ref=slots.at[me],
            send_sem=chi_send.at[source],
            recv_sem=chi_recv.at[me],
            device_id=(source, seg),
            device_id_type=MESH,
        )

    def group(delta, between):
        spread(place, held, rot_ref, turned, nat, sre, sim, delta)
        requests(place, held, wanted, meta, meta_sem, delta)

        @pl.loop(0, 2)
        def _(part):
            for n in range(4):
                slot = part * 4 + n
                source = place.member(delta, slot)
                veto(w0_ref, far_ref, tn, meta, turned, masks, pick, weight, chi, slot, source)

        @pl.loop(0, 8)
        def _(k):
            source = place.member(delta, k)

            @pl.when(source != me)
            def _():
                result(source).start()

        @pl.loop(0, 4)
        def _(step):
            filters(place, table_ref, tmf, itp, sre, sim, lhs, snr_ref, peak, delta, step * 4)
            if between is not None:
                between(step)

    group(0, lambda step: place.onward(step + step // 2 * (1 - 2 * (step % 2))))

    @pl.loop(0, 2)
    def _(n):
        group(1 + 2 * n, None)

    place.last()
    group(2, None)

    slots[pl.ds(me, 1)] = chi[pl.ds(me, 1)]
    tops[...] = jnp.concatenate([jnp.max(peak[m], axis=0, keepdims=True) for m in range(NT)], 0)
    pairs = [
        pltpu.make_async_remote_copy(
            src_ref=tops,
            dst_ref=peaks.at[j],
            send_sem=pair_send.at[j],
            recv_sem=pair_recv.at[j],
            device_id=(me, (seg + j) % 4),
            device_id_type=MESH,
        )
        for j in range(1, 4)
    ]
    for copy in pairs:
        copy.start()

    @pl.loop(0, 32)
    def _(other):
        @pl.when(other != me)
        def _():
            pltpu.make_async_remote_copy(
                src_ref=chi.at[other],
                dst_ref=slots.at[other],
                send_sem=chi_send.at[other],
                recv_sem=chi_recv.at[other],
                device_id=(other, seg),
                device_id_type=MESH,
            ).wait()

    i, j = iota((64, 64), 0), iota((64, 64), 1)
    across = own_ref[...]
    owner = jnp.sum(jnp.where(i == j, across, 0), axis=1, keepdims=True)
    rank = jnp.sum(jnp.where((j < i) & (across == owner), 1, 0), axis=1, keepdims=True)
    choose = jnp.where(iota((64, 256), 1) == owner * 8 + rank, 1.0, 0.0)
    out_ref[...] = jnp.dot(
        choose, slots[...].reshape(256, 128), preferred_element_type=F32, precision=lax.Precision.HIGHEST
    )
    place.finish()
    for copy in pairs:
        copy.wait()
    top = jnp.maximum(jnp.maximum(tops[...], peaks[1]), jnp.maximum(peaks[2], peaks[3]))
    top = jnp.max(top, axis=1, keepdims=True)
    loud = jnp.max(jnp.where(iota((NT, 128), 0) == iota((NT, 128), 1), top, 0.0), axis=0, keepdims=True)
    loud_ref[...] = loud[:, :NT]


def body(
    spectra, templates, bounds, trigger_owner, trigger_template, trigger_segment, trigger_block
):
    vmem = pl.BlockSpec(memory_space=pltpu.VMEM)
    smem = pl.BlockSpec(memory_space=pltpu.SMEM)
    dma = pltpu.SemaphoreType.DMA
    snr, loud, chisq = pl.pallas_call(
        kernel,
        out_shape=(
            jax.ShapeDtypeStruct((NT, 128, 128), F32),
            jax.ShapeDtypeStruct((1, NT), F32),
            jax.ShapeDtypeStruct((64, 128), F32),
        ),
        in_specs=[vmem, vmem, smem] + [vmem] * 8,
        out_specs=(vmem, vmem, vmem),
        scratch_shapes=[
            pltpu.VMEM((32, ROWS, 128), BF),
            pltpu.VMEM((16, 128), F32),
            pltpu.VMEM((2, NT, F), F32),
            pltpu.VMEM((2, NT, 32, 128), BF),
            pltpu.VMEM((NT, 128), F32),
            pltpu.VMEM((NT, 3, 32, 128), BF),
            pltpu.VMEM((NT, 48, 192), BF),
            pltpu.VMEM((NT, 48, 128), F32),
            pltpu.VMEM((8, 8, 32, 128), BF),
            pltpu.VMEM((2, 4, 288, 128), F32),
            pltpu.VMEM((32, F), F32),
            pltpu.VMEM((32, F), F32),
            pltpu.VMEM((256, F), BF),
            pltpu.VMEM((NT, 8, 128), F32),
            pltpu.VMEM((8, 128), I32),
            pltpu.SMEM((8, 128), I32),
            pltpu.VMEM((32, 8, 128), F32),
            pltpu.VMEM((32, 8, 128), F32),
            pltpu.VMEM((NT, 128), F32),
            pltpu.VMEM((4, NT, 128), F32),
            dma((21,)),
            dma((2, 10)),
            dma((2, 32)),
            dma,
            dma((32,)),
            dma((32,)),
            dma((4,)),
            dma((4,)),
        ],
        compiler_params=pltpu.CompilerParams(
            collective_id=0, has_side_effects=True, vmem_limit_bytes=48 * 1024 * 1024
        ),
        name="search",
    )(
        spectra.reshape(2, 2, 2, F),
        templates,
        bounds,
        trigger_owner.reshape(1, 64),
        trigger_template.reshape(1, 64),
        trigger_segment.reshape(1, 64),
        trigger_block.reshape(1, 64),
        *tables(),
    )
    snr = snr.reshape(NT, 32, 2, 2, 128).transpose(0, 1, 3, 2, 4).reshape(NT, 32, 2, 256)
    return snr, loud.reshape(NT), chisq


def solution(mesh):
    in_specs = (
        P(None, None, "tmpl", "seg", None),
        P(None, "tmpl", None),
        P("tmpl", None),
        P(("tmpl", "seg"), None),
        P(("tmpl", "seg")),
        P(("tmpl", "seg")),
        P(("tmpl", "seg")),
    )
    out_specs = (P("tmpl", None, "seg", None), P("tmpl"), P(("tmpl", "seg"), None))
    return jax.shard_map(body, mesh=mesh, in_specs=in_specs, out_specs=out_specs, check_vma=False)
```

time: 365 us -> 73.3 us (0.20)
  matrix products: 145 us -> 0 us
  blocking collectives: 105 us -> 0 us
  Pallas kernels: 0 us -> 60.3 us
  other arithmetic: 49.6 us -> 0 us
  local copies, waits for them, and re-layouts: 47.9 us -> 11.2 us
  between operations: 14.2 us -> 0.66 us
    dot_general x12 -> x0, matrix products: 122 us -> none  [the longest x1 27.9 us: body(): jnp.dot(prod_im, sin_full, preferred_element_type=jnp.float32)]
    all_gather x1 -> x0, blocking collectives: 98.2 us -> none  [body(): lax.all_gather(bounds, 'tmpl', axis=0, tiled=True)]
    pallas_call x0 -> x1, Pallas kernels: none -> 60.3 us  [body(): pl.pallas_call(kernel, out_shape=(jax.ShapeDtypeStruct((NT, 128, 128), F3...]
    gather x10 -> x0, local copies, waits for them, and re-layouts: 29.7 us -> none  [the longest x4 17.8 us: one_group(): jnp.take(bank, group_ids, axis=1)]
    convert_element_type x14 -> x0, other arithmetic: 28.2 us -> none  [the longest x1 19.7 us: wave_table(): jnp.sin(angles).astype(jnp.bfloat16)]
    mul x8 -> x0, matrix products: 23.1 us -> none  [the longest x4 12.9 us: chi_square(): diff_im = corr_im - weight * whole_im]
    pmax x1 -> x0, blocking collectives: 6.39 us -> none  [body(): loudest = lax.pmax(jnp.max(network_snr, axis=(1, 2, 3)), 'seg')]
    reduce_sum x11 -> x0, other arithmetic: 6.18 us -> none  [the longest x5 3.3 us: band_split(): jnp.sum(jnp.where(bin_mask, energy[:, None, :], 0.0), axis=2) + EPSILON]
  transfers between devices with their start and end apart: 2 -> 0, of which waited for: 0 -> 0; matrix products, arithmetic and copies ran while one was open for 43% -> 0% of each run, Pallas kernels for 0% -> 0%
where the time goes in v2:
time: 73.3 us; the launch traced here: 72.1 us
  Pallas kernels  60.3 us (82%)
  local copies, waits for them, and re-layouts  11.2 us (15%)
    pallas_call x1, Pallas kernels, body(): pl.pallas_call(kernel, out_shape=(jax.ShapeDtypeStruct((NT, 128, 128), F3...  60.3 us
    unnamed x25, local copies, waits for them, and re-layouts  11.2 us

profile of v2, /device:TPU:0, one launch (start us, length us, event | category | flops | bytes accessed | tf_op | source)
XLA Modules:
  0.0 72.1 jit_solution(15230919197647148175)
XLA Ops:
  0.6 0.0 copy-start
  0.6 1.6 %copy-done = bf16[4096,256]{1,0:T(8,128)(2,1)S(1)} copy-done((bf16[4096,256]{1,0:T(8,128)(2,1)S(1)}, bf16[4096,256]{1,0:T(8,128)(2,1)}, u32[]{:S(2)}) %copy-start) | copy-done | bytes 2097176
  2.2 0.0 copy-start.1
  2.2 0.9 %copy-done.1 = bf16[2,16,4096]{2,1,0:T(8,128)(2,1)S(1)} copy-done((bf16[2,16,4096]{2,1,0:T(8,128)(2,1)S(1)}, bf16[2,16,4096]{2,1,0:T(8,128)(2,1)}, u32[]{:S(2)}) %copy-start.1) | copy-done | bytes 262168
  3.2 0.0 copy-start.2
  3.2 0.9 %copy-done.2 = bf16[256,256]{1,0:T(8,128)(2,1)S(1)} copy-done((bf16[256,256]{1,0:T(8,128)(2,1)S(1)}, bf16[256,256]{1,0:T(8,128)(2,1)}, u32[]{:S(2)}) %copy-start.2) | copy-done | bytes 131096
  4.1 0.0 copy-start.3
  4.1 0.8 %copy-done.3 = bf16[2,2,1,2,4096]{4,3,2,1,0:T(2,128)(2,1)S(1)} copy-done((bf16[2,2,1,2,4096]{4,3,2,1,0:T(2,128)(2,1)S(1)}, bf16[2,2,1,2,4096]{4,3,2,1,0:T(2,128)(2,1)}, u32[]{:S(2)}) %copy-start.3) | copy-done | bytes 65560
  4.9 0.0 copy-start.4
  4.9 0.8 %copy-done.4 = f32[2,32,128]{2,1,0:T(8,128)S(1)} copy-done((f32[2,32,128]{2,1,0:T(8,128)S(1)}, f32[2,32,128]{2,1,0:T(8,128)}, u32[]{:S(2)}) %copy-start.4) | copy-done | bytes 32792
  5.7 0.0 copy-start.5
  5.7 0.7 copy-done.5
  6.4 0.0 copy-start.6
  6.4 0.7 copy-done.6
  7.1 0.0 copy-start.7
  7.1 0.7 copy-done.7
  7.8 0.0 copy-start.8
  7.8 0.7 copy-done.8
  8.4 0.0 copy-start.9
  8.4 0.7 copy-done.9
  9.1 0.0 copy-start.10
  9.1 0.7 copy-done.10
  9.7 60.3 %search.1 = (f32[16,128,128]{2,1,0:T(8,128)S(1)}, f32[1,16]{1,0:T(1,128)S(1)}, f32[64,128]{1,0:T(8,128)S(1)}) custom-call(bf16[2,2,2,4096]{3,2,1,0:T(2,128)(2,1)S(1)} %bitcast.12, bf16[2,16,4096]{2,1,0:T(8,128)(2,1)S(1)} %copy-done.1, s32[16,15]{1,0:T(8,128)S(1)} %copy-done.6, s32[1,64]{1,0:T(1,128)S(1)} %bitcast.13, s32[1,64]{1,0:T(1,128)S(1)} %bitcast.14, ...), custom_call_target="tpu_custom_call" | custom-call | tf_op jit(solution)/shard_map/search/pallas_call | solution.py:464
  70.0 1.0 %copy.18 = f32[16,32,2,256]{3,2,1,0:T(2,128)} copy(f32[16,32,2,256]{3,2,1,0:T(2,128)S(1)} %bitcast.11) | data formatting | bytes 2097152
  71.0 0.5 copy.19
  71.5 0.6 copy.20
Async XLA Ops:
  0.6 1.6 %copy-start = (bf16[4096,256]{1,0:T(8,128)(2,1)S(1)}, bf16[4096,256]{1,0:T(8,128)(2,1)}, u32[]{:S(2)}) copy-start(bf16[4096,256]{1,0:T(8,128)(2,1)} %constant.19.table_ref) | copy-start | bytes 6291460
  2.2 0.9 %copy-start.1 = (bf16[2,16,4096]{2,1,0:T(8,128)(2,1)S(1)}, bf16[2,16,4096]{2,1,0:T(8,128)(2,1)}, u32[]{:S(2)}) copy-start(bf16[2,16,4096]{2,1,0:T(8,128)(2,1)} %tm_ref.1) | copy-start | bytes 786436
  3.2 0.9 %copy-start.2 = (bf16[256,256]{1,0:T(8,128)(2,1)S(1)}, bf16[256,256]{1,0:T(8,128)(2,1)}, u32[]{:S(2)}) copy-start(bf16[256,256]{1,0:T(8,128)(2,1)} %constant.20.w0_ref) | copy-start | bytes 393220
  4.1 0.8 %copy-start.3 = (bf16[2,2,1,2,4096]{4,3,2,1,0:T(2,128)(2,1)S(1)}, bf16[2,2,1,2,4096]{4,3,2,1,0:T(2,128)(2,1)}, u32[]{:S(2)}) copy-start(bf16[2,2,1,2,4096]{4,3,2,1,0:T(2,128)(2,1)} %param.11) | copy-start | bytes 196612
  4.9 0.8 %copy-start.4 = (f32[2,32,128]{2,1,0:T(8,128)S(1)}, f32[2,32,128]{2,1,0:T(8,128)}, u32[]{:S(2)}) copy-start(f32[2,32,128]{2,1,0:T(8,128)} %constant.9.clone.rot_ref) | copy-start | bytes 98308
  5.7 0.7 copy-start.5
  6.4 0.7 copy-start.6
  7.1 0.7 copy-start.7
  7.8 0.7 copy-start.8
  8.4 0.7 copy-start.9
  9.1 0.7 copy-start.10

commit v3 on v2

--- a/solution.py
+++ b/solution.py
@@ -107,12 +107,15 @@
     def first(self):
         self.arrive(self.step(1, 0, 0))
         self.sides(1)
-        self.fan(1, 0)
-        for near in (1, 3):
-            for kind in (0, 1):
+        for kind in (0, 1):
+            for near in (1, 3):
                 source = self.step(kind, near, 0)
                 self.arrive(source)
                 self.copy(source, self.step(kind, 4 - near, 0, True), 1 if near == 1 else 0, kind).start()
+            if kind == 0:
+                self.fan(1, 0)
+        for kind in (0, 1):
+            for near in (1, 3):
                 self.fan(kind, near)
         for kind in (0, 1):
             self.arrive(self.step(kind, 2, 0), True)
@@ -260,7 +263,7 @@
     wanted[...] = table.astype(I32)
     copy = pltpu.make_async_copy(wanted, meta, sem)
     copy.start()
-    copy.wait()
+    return copy
 
 
 def veto(w0_ref, far_ref, tn, meta, turned, masks, pick, weight, chi, slot, source):
@@ -342,15 +345,21 @@
 
 
 def kernel(
-    spec_ref, tm_ref, bounds_ref, own_ref, tmpl_ref, seg_ref, blk_ref, table_ref, rot_ref, w0_ref, far_ref,
+    spec_in, own_in, tmpl_in, seg_in, blk_in, tm_in, bounds_in, rot_in, w0_in, far_in, table_in,
     snr_ref, loud_ref, out_ref,
+    spec_ref, own_ref, tmpl_ref, seg_ref, blk_ref, tm_ref, bounds_ref, rot_ref, w0_ref, far_ref, table_ref,
     held, listed, tmf, tn, itp, masks, pick, weight, turned, nat, sre, sim, lhs, peak, wanted, meta,
     chi, slots, tops, peaks,
-    full_sem, half_sem, recv_sem, meta_sem, chi_send, chi_recv, pair_send, pair_recv,
+    full_sem, half_sem, recv_sem, meta_sem, chi_send, chi_recv, pair_send, pair_recv, in_sem,
 ):
     place = Torus(held, full_sem, half_sem, recv_sem)
     me, seg = place.me, place.seg
     barrier = pltpu.get_barrier_semaphore()
+    given = (spec_in, own_in, tmpl_in, seg_in, blk_in, tm_in, bounds_in, rot_in, w0_in, far_in, table_in)
+    kept = (spec_ref, own_ref, tmpl_ref, seg_ref, blk_ref, tm_ref, bounds_ref, rot_ref, w0_ref, far_ref, table_ref)
+    inputs = [pltpu.make_async_copy(a, b, in_sem.at[n]) for n, (a, b) in enumerate(zip(given, kept))]
+    for copy in inputs:
+        copy.start()
 
     @pl.loop(1, 32)
     def _(j):
@@ -358,9 +367,13 @@
 
     for j in range(1, 4):
         pl.semaphore_signal(barrier, inc=1, device_id=(me, (seg + j) % 4), device_id_type=MESH)
+    for copy in inputs[:5]:
+        copy.wait()
     lay_out(spec_ref, own_ref, tmpl_ref, seg_ref, blk_ref, tm_ref, held, tn, nat, listed, me)
     pl.semaphore_wait(barrier, 34)
     place.begin()
+    for copy in inputs[5:]:
+        copy.wait()
     prepare(tm_ref, bounds_ref, tmf, tn, nat, itp, masks, pick, weight)
     peak[...] = jnp.zeros_like(peak)
     place.first()
@@ -376,8 +389,9 @@
         )
 
     def group(delta, between):
+        asked = requests(place, held, wanted, meta, meta_sem, delta)
         spread(place, held, rot_ref, turned, nat, sre, sim, delta)
-        requests(place, held, wanted, meta, meta_sem, delta)
+        asked.wait()
 
         @pl.loop(0, 2)
         def _(part):
@@ -459,8 +473,8 @@
     spectra, templates, bounds, trigger_owner, trigger_template, trigger_segment, trigger_block
 ):
     vmem = pl.BlockSpec(memory_space=pltpu.VMEM)
-    smem = pl.BlockSpec(memory_space=pltpu.SMEM)
     dma = pltpu.SemaphoreType.DMA
+    wave, rot, w0, far = tables()
     snr, loud, chisq = pl.pallas_call(
         kernel,
         out_shape=(
@@ -468,9 +482,20 @@
             jax.ShapeDtypeStruct((1, NT), F32),
             jax.ShapeDtypeStruct((64, 128), F32),
         ),
-        in_specs=[vmem, vmem, smem] + [vmem] * 8,
+        in_specs=[pl.BlockSpec(memory_space=pltpu.HBM)] * 11,
         out_specs=(vmem, vmem, vmem),
         scratch_shapes=[
+            pltpu.VMEM((2, 2, 2, F), BF),
+            pltpu.VMEM((1, 64), I32),
+            pltpu.VMEM((1, 64), I32),
+            pltpu.VMEM((1, 64), I32),
+            pltpu.VMEM((1, 64), I32),
+            pltpu.VMEM((2, NT, F), BF),
+            pltpu.SMEM((NT, 15), I32),
+            pltpu.VMEM((2, 32, 128), F32),
+            pltpu.VMEM((256, 256), BF),
+            pltpu.VMEM((2, 32, 128), BF),
+            pltpu.VMEM((F, 256), BF),
             pltpu.VMEM((32, ROWS, 128), BF),
             pltpu.VMEM((16, 128), F32),
             pltpu.VMEM((2, NT, F), F32),
@@ -499,20 +524,24 @@
             dma((32,)),
             dma((4,)),
             dma((4,)),
+            dma((11,)),
         ],
         compiler_params=pltpu.CompilerParams(
-            collective_id=0, has_side_effects=True, vmem_limit_bytes=48 * 1024 * 1024
+            collective_id=0, has_side_effects=True, vmem_limit_bytes=62 * 1024 * 1024
         ),
         name="search",
     )(
         spectra.reshape(2, 2, 2, F),
-        templates,
-        bounds,
         trigger_owner.reshape(1, 64),
         trigger_template.reshape(1, 64),
         trigger_segment.reshape(1, 64),
         trigger_block.reshape(1, 64),
-        *tables(),
+        templates,
+        bounds,
+        rot,
+        w0,
+        far,
+        wave,
     )
     snr = snr.reshape(NT, 32, 2, 2, 128).transpose(0, 1, 3, 2, 4).reshape(NT, 32, 2, 256)
     return snr, loud.reshape(NT), chisq

time: 73.3 us -> 61.2 us (0.83)
  local copies, waits for them, and re-layouts: 11.2 us -> 3.79 us
  Pallas kernels: 60.3 us -> 55.8 us
    unnamed x25 -> x7, local copies, waits for them, and re-layouts: 11.2 us -> 3.79 us
    pallas_call x1, Pallas kernels: 60.3 us -> 55.8 us  [body(): pl.pallas_call(kernel, out_shape=(jax.ShapeDtypeStruct((NT, 128, 128), F3...]
where the time goes in v3:
time: 61.2 us; the launch traced here: 60.2 us
  Pallas kernels  55.8 us (91%)
  local copies, waits for them, and re-layouts  3.79 us (6%)
  between operations  0.66 us (1%)
    pallas_call x1, Pallas kernels, body(): pl.pallas_call(kernel, out_shape=(jax.ShapeDtypeStruct((NT, 128, 128), F3...  55.8 us
    unnamed x7, local copies, waits for them, and re-layouts  3.79 us

profile of v3, /device:TPU:0, one launch (start us, length us, event | category | flops | bytes accessed | tf_op | source)
XLA Modules:
  0.0 60.2 jit_solution(900038055588497800)
XLA Ops:
  0.6 55.8 %search.1 = (f32[16,128,128]{2,1,0:T(8,128)}, f32[1,16]{1,0:T(1,128)}, f32[64,128]{1,0:T(8,128)}) custom-call(bf16[2,2,2,4096]{3,2,1,0:T(2,128)(2,1)} %bitcast.12, s32[1,64]{1,0:T(1,128)} %bitcast.13, s32[1,64]{1,0:T(1,128)} %bitcast.14, s32[1,64]{1,0:T(1,128)} %bitcast.15, s32[1,64]{1,0:T(1,128)} %bitcast.16, bf16[2,16,4096]{2,1,0:T(8,128)(2,1)} %tm_in.1, ...), custom_call_target="tpu_custom_call" | custom-call | tf_op jit(solution)/shard_map/search/pallas_call | solution.py:478
  56.4 0.0 copy-start.1
  56.4 0.0 copy-start
  56.4 2.7 %copy.18 = f32[16,32,2,256]{3,2,1,0:T(2,128)} copy(f32[16,32,2,256]{3,2,1,0:T(2,128)} %bitcast.11) | data formatting | bytes 2097152
  59.1 0.0 copy-done.1
  59.1 0.5 copy.19
  59.6 0.0 copy-done
  59.6 0.6 %copy.20 = f32[64,128]{1,0:T(8,128)} copy(f32[64,128]{1,0:T(8,128)S(1)} %copy-done) | data formatting | bytes 65536
Async XLA Ops:
  56.4 2.7 %copy-start.1 = (f32[1,16]{1,0:T(1,128)S(1)}, f32[1,16]{1,0:T(1,128)}, u32[]{:S(2)}) copy-start(f32[1,16]{1,0:T(1,128)} %get-tuple-element.7) | copy-start | bytes 196
  56.4 3.2 %copy-start = (f32[64,128]{1,0:T(8,128)S(1)}, f32[64,128]{1,0:T(8,128)}, u32[]{:S(2)}) copy-start(f32[64,128]{1,0:T(8,128)} %get-tuple-element.14) | copy-start | bytes 98308

commit v4 on v3

--- a/solution.py
+++ b/solution.py
@@ -104,9 +104,15 @@
         self.sides(0)
         self.fan(0, 0)
 
-    def first(self):
-        self.arrive(self.step(1, 0, 0))
+    def place_of(self, source):
+        plane = source // 16
+        return plane * (4 + source % 4) + (1 - plane) * (source // 4 % 4)
+
+    def first(self, work):
+        mate = self.step(1, 0, 0)
+        self.arrive(mate)
         self.sides(1)
+        work([self.me, mate])
         for kind in (0, 1):
             for near in (1, 3):
                 source = self.step(kind, near, 0)
@@ -117,9 +123,11 @@
         for kind in (0, 1):
             for near in (1, 3):
                 self.fan(kind, near)
+        work([self.step(kind, near, 0) for kind in (0, 1) for near in (1, 3)])
         for kind in (0, 1):
             self.arrive(self.step(kind, 2, 0), True)
             self.fan(kind, 2)
+        work([self.step(kind, 2, 0) for kind in (0, 1)])
 
     def onward(self, near):
         for kind in (0, 1):
@@ -225,55 +233,54 @@
             masks[m, q] = jnp.where(index == q, 1.0, 0.0).astype(BF)
 
 
-def spread(place, held, rot_ref, turned, nat, sre, sim, delta):
+def turn(held, rot_ref, turned, nat, source, k):
     rc, rs = rot_ref[0], rot_ref[1]
-
-    @pl.loop(0, 8)
-    def _(k):
-        a = place.member(delta, k)
-        for q in range(4):
-            re = held[a, pl.ds(32 * q, 32), :].astype(F32)
-            im = held[a, pl.ds(ROWS_A + 32 * q, 32), :].astype(F32)
-            tr = re * rc - im * rs
-            ti = re * rs + im * rc
-            turned[k, q] = tr.astype(BF)
-            turned[k, 4 + q] = ti.astype(BF)
-            nat[0, q, pl.ds(k * 32, 32), :] = tr
-            nat[1, q, pl.ds(k * 32, 32), :] = ti
-
+    for q in range(4):
+        re = held[source, pl.ds(32 * q, 32), :].astype(F32)
+        im = held[source, pl.ds(ROWS_A + 32 * q, 32), :].astype(F32)
+        tr = re * rc - im * rs
+        ti = re * rs + im * rc
+        turned[k, q] = tr.astype(BF)
+        turned[k, 4 + q] = ti.astype(BF)
+        nat[0, q, pl.ds(pl.multiple_of(k * 32, 32), 32), :] = tr
+        nat[1, q, pl.ds(pl.multiple_of(k * 32, 32), 32), :] = ti
+
+
+def spread(nat, sre, sim):
     for q in range(4):
         for c in range(32):
             sre[pl.ds(8 * q, 8), pl.ds(c * 128, 128)] = nat[0, q, pl.ds(c, 8, stride=32), :]
             sim[pl.ds(8 * q, 8), pl.ds(c * 128, 128)] = nat[1, q, pl.ds(c, 8, stride=32), :]
 
 
-def requests(place, held, wanted, meta, sem, delta):
+def requests(place, held, wanted, meta, sem, sources):
     shard = place.me.astype(F32)
-    tiles = [held[place.member(delta, k), pl.ds(128, 16), :].astype(F32) for k in range(8)]
+    tiles = [held[source, pl.ds(128, 16), :].astype(F32) for source in sources]
+    tiles = tiles + tiles[:1] * (8 - len(tiles))
     rows = [jnp.concatenate([t[v : v + 1] for t in tiles], 0) for v in range(4)]
     lane = iota((8, 128), 1)
     hit = (rows[0] == shard) & (lane < 64)
     before = jnp.where(iota((128, 128), 0) < iota((128, 128), 1), 1.0, 0.0).astype(BF)
     rank = jnp.dot(jnp.where(hit, 1.0, 0.0).astype(BF), before, preferred_element_type=F32)
+    terms = [jnp.where(hit & (rank == float(k)), rows[v + 1], 0.0) for v in range(3) for k in range(4)]
+    sums = jnp.dot(jnp.concatenate(terms, 0).astype(BF), jnp.ones((128, 128), BF), preferred_element_type=F32)
     table = jnp.zeros((8, 128), F32)
-    for v in range(3):
-        for k in range(4):
-            value = jnp.sum(jnp.where(hit & (rank == float(k)), rows[v + 1], 0.0), axis=1, keepdims=True)
-            table = jnp.where(lane == 4 * v + k, value, table)
+    for n in range(12):
+        table = jnp.where(lane == n, sums[8 * n : 8 * n + 8], table)
     wanted[...] = table.astype(I32)
     copy = pltpu.make_async_copy(wanted, meta, sem)
     copy.start()
     return copy
 
 
-def veto(w0_ref, far_ref, tn, meta, turned, masks, pick, weight, chi, slot, source):
+def veto(w0_ref, far_ref, tn, meta, turned, masks, pick, weight, chi, row, slot, source):
     fc, fs = far_ref[0], far_ref[1]
     rows = []
     at = []
     for k in range(4):
-        m = jnp.clip(meta[slot, k], 0, NT - 1)
-        r = jnp.clip(meta[slot, 4 + k], 0, 1)
-        blk = jnp.clip(meta[slot, 8 + k], 0, 1)
+        m = jnp.clip(meta[row, k], 0, NT - 1)
+        r = jnp.clip(meta[row, 4 + k], 0, 1)
+        blk = jnp.clip(meta[row, 8 + k], 0, 1)
         at.append((m, blk))
         h0, h1 = tn[0, m], tn[1, m]
         sign = (2 * blk - 1).astype(F32).astype(BF)
@@ -304,7 +311,7 @@
     late = jnp.zeros((8, 128), I32)
     for k in range(4):
         late = jnp.where(sub == k, lines[k][0], late)
-    chi[source] = jnp.where(late == 1, value, back)
+    chi[source // 4 % 4, source // 16, source % 4] = jnp.where(late == 1, value, back)
 
 
 def filters(place, table_ref, tmf, itp, sre, sim, lhs, snr_ref, peak, delta, first):
@@ -349,7 +356,7 @@
     snr_ref, loud_ref, out_ref,
     spec_ref, own_ref, tmpl_ref, seg_ref, blk_ref, tm_ref, bounds_ref, rot_ref, w0_ref, far_ref, table_ref,
     held, listed, tmf, tn, itp, masks, pick, weight, turned, nat, sre, sim, lhs, peak, wanted, meta,
-    chi, slots, tops, peaks,
+    chi, over_x, over_y, slots, tops, peaks,
     full_sem, half_sem, recv_sem, meta_sem, chi_send, chi_recv, pair_send, pair_recv, in_sem,
 ):
     place = Torus(held, full_sem, half_sem, recv_sem)
@@ -361,36 +368,38 @@
     for copy in inputs:
         copy.start()
 
-    @pl.loop(1, 32)
-    def _(j):
-        pl.semaphore_signal(barrier, inc=1, device_id=((me + j) % 32, seg), device_id_type=MESH)
-
-    for j in range(1, 4):
-        pl.semaphore_signal(barrier, inc=1, device_id=(me, (seg + j) % 4), device_id_type=MESH)
+    z, x, y = place.z, place.x, place.y
+    friends = [(ring(1 - z, x, y), seg)]
+    for j in (1, 3, 2):
+        friends += [(ring(z, x + j, y), seg), (ring(z, x, y + j), seg)]
+    friends += [(me, (seg + j) % 4) for j in range(1, 4)]
+    for friend in friends:
+        pl.semaphore_signal(barrier, inc=1, device_id=friend, device_id_type=MESH)
     for copy in inputs[:5]:
         copy.wait()
     lay_out(spec_ref, own_ref, tmpl_ref, seg_ref, blk_ref, tm_ref, held, tn, nat, listed, me)
-    pl.semaphore_wait(barrier, 34)
+    pl.semaphore_wait(barrier, 10)
     place.begin()
     for copy in inputs[5:]:
         copy.wait()
     prepare(tm_ref, bounds_ref, tmf, tn, nat, itp, masks, pick, weight)
     peak[...] = jnp.zeros_like(peak)
-    place.first()
-
-    def result(source):
-        return pltpu.make_async_remote_copy(
-            src_ref=chi.at[source],
-            dst_ref=slots.at[me],
-            send_sem=chi_send.at[source],
-            recv_sem=chi_recv.at[me],
-            device_id=(source, seg),
-            device_id_type=MESH,
-        )
-
-    def group(delta, between):
-        asked = requests(place, held, wanted, meta, meta_sem, delta)
-        spread(place, held, rot_ref, turned, nat, sre, sim, delta)
+
+    def work(sources):
+        asked = requests(place, held, wanted, meta, meta_sem, sources)
+        for source in sources:
+            turn(held, rot_ref, turned, nat, source, place.place_of(source))
+        asked.wait()
+        for row, source in enumerate(sources):
+            veto(w0_ref, far_ref, tn, meta, turned, masks, pick, weight, chi, row, place.place_of(source), source)
+
+    def serve(delta):
+        asked = requests(place, held, wanted, meta, meta_sem, [place.member(delta, k) for k in range(8)])
+
+        @pl.loop(0, 8)
+        def _(k):
+            turn(held, rot_ref, turned, nat, place.member(delta, k), k)
+
         asked.wait()
 
         @pl.loop(0, 2)
@@ -398,15 +407,10 @@
             for n in range(4):
                 slot = part * 4 + n
                 source = place.member(delta, slot)
-                veto(w0_ref, far_ref, tn, meta, turned, masks, pick, weight, chi, slot, source)
-
-        @pl.loop(0, 8)
-        def _(k):
-            source = place.member(delta, k)
-
-            @pl.when(source != me)
-            def _():
-                result(source).start()
+                veto(w0_ref, far_ref, tn, meta, turned, masks, pick, weight, chi, slot, slot, source)
+
+    def scan(delta, between):
+        spread(nat, sre, sim)
 
         @pl.loop(0, 4)
         def _(step):
@@ -414,16 +418,57 @@
             if between is not None:
                 between(step)
 
-    group(0, lambda step: place.onward(step + step // 2 * (1 - 2 * (step % 2))))
+    def result(axis, j):
+        if axis == 0:
+            src, dst, peer = chi.at[(x + j) % 4], over_x.at[x], ring(z, x + j, y)
+        elif axis == 1:
+            src, dst, peer = over_x.at[:, :, (y + j) % 4], over_y.at[y], ring(z, x, y + j)
+        else:
+            src, dst, peer = over_y.at[:, :, 1 - z], slots.at[z], ring(1 - z, x, y)
+        return pltpu.make_async_remote_copy(
+            src_ref=src,
+            dst_ref=dst,
+            send_sem=chi_send.at[axis, j],
+            recv_sem=chi_recv.at[axis, j],
+            device_id=(peer, seg),
+            device_id_type=MESH,
+        )
+
+    place.first(work)
+    scan(0, lambda step: place.onward(step + step // 2 * (1 - 2 * (step % 2))))
 
     @pl.loop(0, 2)
     def _(n):
-        group(1 + 2 * n, None)
+        serve(1 + 2 * n)
+        scan(1 + 2 * n, None)
 
     place.last()
-    group(2, None)
-
-    slots[pl.ds(me, 1)] = chi[pl.ds(me, 1)]
+    serve(2)
+    for j in (1, 2, 3):
+        result(0, j).start()
+    over_x[pl.ds(x, 1)] = chi[pl.ds(x, 1)]
+
+    def homeward(step):
+        @pl.when(step == 1)
+        def _():
+            for j in (1, 2, 3):
+                result(0, j).wait()
+            for j in (1, 2, 3):
+                result(1, j).start()
+            for n in range(4):
+                for p in range(2):
+                    over_y[y, n, p] = over_x[n, p, y]
+
+        @pl.when(step == 3)
+        def _():
+            for j in (1, 2, 3):
+                result(1, j).wait()
+            result(2, 0).start()
+            for n in range(4):
+                for p in range(4):
+                    slots[z, n, p] = over_y[n, p, z]
+
+    scan(2, homeward)
     tops[...] = jnp.concatenate([jnp.max(peak[m], axis=0, keepdims=True) for m in range(NT)], 0)
     pairs = [
         pltpu.make_async_remote_copy(
@@ -438,35 +483,47 @@
     ]
     for copy in pairs:
         copy.start()
-
-    @pl.loop(0, 32)
-    def _(other):
-        @pl.when(other != me)
-        def _():
-            pltpu.make_async_remote_copy(
-                src_ref=chi.at[other],
-                dst_ref=slots.at[other],
-                send_sem=chi_send.at[other],
-                recv_sem=chi_recv.at[other],
-                device_id=(other, seg),
-                device_id_type=MESH,
-            ).wait()
-
+    place.finish()
+    result(2, 0).wait()
     i, j = iota((64, 64), 0), iota((64, 64), 1)
     across = own_ref[...]
     owner = jnp.sum(jnp.where(i == j, across, 0), axis=1, keepdims=True)
     rank = jnp.sum(jnp.where((j < i) & (across == owner), 1, 0), axis=1, keepdims=True)
-    choose = jnp.where(iota((64, 256), 1) == owner * 8 + rank, 1.0, 0.0)
+    where = owner // 16 * 16 + owner % 4 * 4 + owner // 4 % 4
+    choose = jnp.where(iota((64, 256), 1) == where * 8 + rank, 1.0, 0.0)
     out_ref[...] = jnp.dot(
         choose, slots[...].reshape(256, 128), preferred_element_type=F32, precision=lax.Precision.HIGHEST
     )
-    place.finish()
     for copy in pairs:
         copy.wait()
     top = jnp.maximum(jnp.maximum(tops[...], peaks[1]), jnp.maximum(peaks[2], peaks[3]))
     top = jnp.max(top, axis=1, keepdims=True)
     loud = jnp.max(jnp.where(iota((NT, 128), 0) == iota((NT, 128), 1), top, 0.0), axis=0, keepdims=True)
     loud_ref[...] = loud[:, :NT]
+
+
+def handed_kernel(*refs):
+    sem = refs[6]
+    copies = [pltpu.make_async_copy(refs[n], refs[n + 3], sem.at[n]) for n in (1, 2)]
+    for n in range(4):
+        cut = pl.ds(4 * n, 4)
+        copies.append(pltpu.make_async_copy(refs[0].at[cut], refs[3].at[cut], sem.at[3 + n]))
+    for copy in copies:
+        copy.start()
+    for copy in copies:
+        copy.wait()
+
+
+def handed(*arrays):
+    hbm = pl.BlockSpec(memory_space=pltpu.HBM)
+    return pl.pallas_call(
+        handed_kernel,
+        out_shape=tuple(jax.ShapeDtypeStruct(a.shape, a.dtype) for a in arrays),
+        in_specs=[hbm] * 3,
+        out_specs=(hbm,) * 3,
+        scratch_shapes=[pltpu.SemaphoreType.DMA((7,))],
+        name="handed",
+    )(*arrays)
 
 
 def body(
@@ -512,16 +569,18 @@
             pltpu.VMEM((NT, 8, 128), F32),
             pltpu.VMEM((8, 128), I32),
             pltpu.SMEM((8, 128), I32),
-            pltpu.VMEM((32, 8, 128), F32),
-            pltpu.VMEM((32, 8, 128), F32),
+            pltpu.VMEM((4, 2, 4, 8, 128), F32),
+            pltpu.VMEM((4, 2, 4, 8, 128), F32),
+            pltpu.VMEM((4, 4, 2, 8, 128), F32),
+            pltpu.VMEM((2, 4, 4, 8, 128), F32),
             pltpu.VMEM((NT, 128), F32),
             pltpu.VMEM((4, NT, 128), F32),
             dma((21,)),
             dma((2, 10)),
             dma((2, 32)),
             dma,
-            dma((32,)),
-            dma((32,)),
+            dma((3, 4)),
+            dma((3, 4)),
             dma((4,)),
             dma((4,)),
             dma((11,)),
@@ -543,6 +602,7 @@
         far,
         wave,
     )
+    snr, loud, chisq = handed(snr, loud, chisq)
     snr = snr.reshape(NT, 32, 2, 2, 128).transpose(0, 1, 3, 2, 4).reshape(NT, 32, 2, 256)
     return snr, loud.reshape(NT), chisq
 

time: 61.2 us -> 93.4 us (1.53)
  Pallas kernels: 55.8 us -> 91.5 us
  local copies, waits for them, and re-layouts: 3.79 us -> 0 us
    pallas_call x0 -> x1, Pallas kernels: none -> 33.9 us  [handed(): pl.pallas_call(handed_kernel, out_shape=tuple((jax.ShapeDtypeStruct(a.sha...]
    unnamed x7 -> x0, local copies, waits for them, and re-layouts: 3.79 us -> none
    pallas_call x1, Pallas kernels: 55.8 us -> 57.5 us  [body(): pl.pallas_call(kernel, out_shape=(jax.ShapeDtypeStruct((NT, 128, 128), F3...]
where the time goes in v4:
time: 93.4 us; the launch traced here: 92.3 us
  Pallas kernels  91.5 us (98%)
    pallas_call x1, Pallas kernels, body(): pl.pallas_call(kernel, out_shape=(jax.ShapeDtypeStruct((NT, 128, 128), F3...  57.5 us
    pallas_call x1, Pallas kernels, handed(): pl.pallas_call(handed_kernel, out_shape=tuple((jax.ShapeDtypeStruct(a.sha...  33.9 us

profile of v4, /device:TPU:0, one launch (start us, length us, event | category | flops | bytes accessed | tf_op | source)
XLA Modules:
  0.0 92.3 jit_solution(13467648767255510364)
XLA Ops:
  0.6 57.5 %search.1 = (f32[16,128,128]{2,1,0:T(8,128)}, f32[1,16]{1,0:T(1,128)}, f32[64,128]{1,0:T(8,128)}) custom-call(bf16[2,2,2,4096]{3,2,1,0:T(2,128)(2,1)} %bitcast.11, s32[1,64]{1,0:T(1,128)} %bitcast.12, s32[1,64]{1,0:T(1,128)} %bitcast.13, s32[1,64]{1,0:T(1,128)} %bitcast.14, s32[1,64]{1,0:T(1,128)} %bitcast.15, bf16[2,16,4096]{2,1,0:T(8,128)(2,1)} %tm_in.1, ...), custom_call_target="tpu_custom_call" | custom-call | tf_op jit(solution)/shard_map/search/pallas_call | solution.py:535
  58.2 33.9 %handed.1 = (f32[16,128,128]{2,1,0:T(8,128)}, f32[1,16]{1,0:T(1,128)}, f32[64,128]{1,0:T(8,128)}) custom-call(f32[16,128,128]{2,1,0:T(8,128)} %get-tuple-element.9.refs_0_, f32[1,16]{1,0:T(1,128)} %get-tuple-element.10.refs_1_, f32[64,128]{1,0:T(8,128)} %get-tuple-element.11.refs_2_), custom_call_target="tpu_custom_call" | custom-call | tf_op jit(solution)/shard_map/handed/pallas_call | solution.py:519

commit v5 on v4

--- a/solution.py
+++ b/solution.py
@@ -62,16 +62,21 @@
         self.held, self.full_sem, self.half_sem, self.recv_sem = held, full_sem, half_sem, recv_sem
 
     def step(self, kind, near, far, here=False):
-        plane = self.z if kind == 0 else 1 - self.z
+        plane = self.z * (1 - kind) + (1 - self.z) * kind
         xx = self.x + near * (1 - plane) + far * plane
         yy = self.y + near * plane + far * (1 - plane)
         return ring(self.z if here else plane, xx, yy)
 
-    def member(self, delta, k):
+    def early(self, k):
         plane, at = k // 4, k % 4
-        first = at * 4 + (self.y + delta) % 4
-        second = 16 + (self.x + delta) % 4 * 4 + at
-        return (1 - plane) * first + plane * second
+        return (1 - plane) * (at * 4 + self.y) + plane * (16 + self.x * 4 + at)
+
+    def beside(self, part, k):
+        one = k // 2 % 2
+        return self.step(k // 4, part * (3 - one) + (1 - part) * one, 1 + 2 * (k % 2))
+
+    def across(self, k):
+        return self.step(k // 4, k % 4, 2)
 
     def copy(self, source, peer, half, sem):
         if half is None:
@@ -311,10 +316,10 @@
     late = jnp.zeros((8, 128), I32)
     for k in range(4):
         late = jnp.where(sub == k, lines[k][0], late)
-    chi[source // 4 % 4, source // 16, source % 4] = jnp.where(late == 1, value, back)
-
-
-def filters(place, table_ref, tmf, itp, sre, sim, lhs, snr_ref, peak, delta, first):
+    chi[source // 4, source % 4] = jnp.where(late == 1, value, back)
+
+
+def filters(place, table_ref, tmf, itp, sre, sim, lhs, snr_ref, peak, member, first):
     for n in range(4):
         for k in range(F // 256):
             cut = pl.ds(k * 256, 256)
@@ -326,8 +331,7 @@
             lhs[pl.ds(64 * n + 32, 32), cut] = (im * h0 - re * h1).astype(BF)
     acc = jnp.dot(lhs[...], table_ref[...], preferred_element_type=F32)
     back = 127 - iota((16, 128), 1)
-    one = (place.y + delta) % 4 * 4
-    two = 64 + (place.x + delta) % 4 * 16
+    bases = [member(k) * 4 for k in range(8)]
     for n in range(4):
         a = acc[64 * n : 64 * n + 32, :128]
         d = acc[64 * n : 64 * n + 32, 128:]
@@ -345,10 +349,9 @@
         for half, value in enumerate((minus, plus)):
             for r in range(2):
                 to = 2 * half + r
-                snr_ref[first + n, pl.ds(one + to, 4, stride=16), :] = value[8 * r : 8 * r + 4]
-                for k in range(4):
-                    line = value[8 * r + 4 + k : 8 * r + 5 + k]
-                    snr_ref[first + n, pl.ds(two + to + 4 * k, 1), :] = line
+                for k in range(8):
+                    line = value[8 * r + k : 8 * r + k + 1]
+                    snr_ref[first + n, pl.ds(bases[k] + to, 1), :] = line
 
 
 def kernel(
@@ -356,7 +359,7 @@
     snr_ref, loud_ref, out_ref,
     spec_ref, own_ref, tmpl_ref, seg_ref, blk_ref, tm_ref, bounds_ref, rot_ref, w0_ref, far_ref, table_ref,
     held, listed, tmf, tn, itp, masks, pick, weight, turned, nat, sre, sim, lhs, peak, wanted, meta,
-    chi, over_x, over_y, slots, tops, peaks,
+    chi, over, slots, tops, peaks,
     full_sem, half_sem, recv_sem, meta_sem, chi_send, chi_recv, pair_send, pair_recv, in_sem,
 ):
     place = Torus(held, full_sem, half_sem, recv_sem)
@@ -369,16 +372,16 @@
         copy.start()
 
     z, x, y = place.z, place.x, place.y
-    friends = [(ring(1 - z, x, y), seg)]
-    for j in (1, 3, 2):
-        friends += [(ring(z, x + j, y), seg), (ring(z, x, y + j), seg)]
+    plane = me // 4
+    friends = [(((plane + j) % 8) * 4 + y, seg) for j in range(1, 8)]
+    friends += [(ring(z, x, y + j), seg) for j in range(1, 4)]
     friends += [(me, (seg + j) % 4) for j in range(1, 4)]
     for friend in friends:
         pl.semaphore_signal(barrier, inc=1, device_id=friend, device_id_type=MESH)
     for copy in inputs[:5]:
         copy.wait()
     lay_out(spec_ref, own_ref, tmpl_ref, seg_ref, blk_ref, tm_ref, held, tn, nat, listed, me)
-    pl.semaphore_wait(barrier, 10)
+    pl.semaphore_wait(barrier, 13)
     place.begin()
     for copy in inputs[5:]:
         copy.wait()
@@ -393,12 +396,12 @@
         for row, source in enumerate(sources):
             veto(w0_ref, far_ref, tn, meta, turned, masks, pick, weight, chi, row, place.place_of(source), source)
 
-    def serve(delta):
-        asked = requests(place, held, wanted, meta, meta_sem, [place.member(delta, k) for k in range(8)])
+    def serve(member):
+        asked = requests(place, held, wanted, meta, meta_sem, [member(k) for k in range(8)])
 
         @pl.loop(0, 8)
         def _(k):
-            turn(held, rot_ref, turned, nat, place.member(delta, k), k)
+            turn(held, rot_ref, turned, nat, member(k), k)
 
         asked.wait()
 
@@ -406,25 +409,22 @@
         def _(part):
             for n in range(4):
                 slot = part * 4 + n
-                source = place.member(delta, slot)
-                veto(w0_ref, far_ref, tn, meta, turned, masks, pick, weight, chi, slot, slot, source)
-
-    def scan(delta, between):
+                veto(w0_ref, far_ref, tn, meta, turned, masks, pick, weight, chi, slot, slot, member(slot))
+
+    def scan(member, between):
         spread(nat, sre, sim)
 
         @pl.loop(0, 4)
         def _(step):
-            filters(place, table_ref, tmf, itp, sre, sim, lhs, snr_ref, peak, delta, step * 4)
-            if between is not None:
-                between(step)
+            filters(place, table_ref, tmf, itp, sre, sim, lhs, snr_ref, peak, member, step * 4)
+            between(step)
 
     def result(axis, j):
         if axis == 0:
-            src, dst, peer = chi.at[(x + j) % 4], over_x.at[x], ring(z, x + j, y)
-        elif axis == 1:
-            src, dst, peer = over_x.at[:, :, (y + j) % 4], over_y.at[y], ring(z, x, y + j)
+            to = (plane + j) % 8
+            src, dst, peer = chi.at[to], over.at[plane], to * 4 + y
         else:
-            src, dst, peer = over_y.at[:, :, 1 - z], slots.at[z], ring(1 - z, x, y)
+            src, dst, peer = over.at[:, (y + j) % 4], slots.at[y], ring(z, x, y + j)
         return pltpu.make_async_remote_copy(
             src_ref=src,
             dst_ref=dst,
@@ -435,40 +435,47 @@
         )
 
     place.first(work)
-    scan(0, lambda step: place.onward(step + step // 2 * (1 - 2 * (step % 2))))
+
+    def pass_on(step):
+        @pl.when(step == 2)
+        def _():
+            place.onward(0)
+
+    scan(place.early, pass_on)
+    place.onward(1)
 
     @pl.loop(0, 2)
-    def _(n):
-        serve(1 + 2 * n)
-        scan(1 + 2 * n, None)
+    def _(part):
+        serve(lambda k: place.beside(part, k))
+
+        @pl.when(part == 0)
+        def _():
+            place.onward(3)
+
+        def pass_more(step):
+            @pl.when((step == 2) & (part == 0))
+            def _():
+                place.onward(2)
+
+        scan(lambda k: place.beside(part, k), pass_more)
 
     place.last()
-    serve(2)
-    for j in (1, 2, 3):
+    serve(place.across)
+    for j in range(1, 8):
         result(0, j).start()
-    over_x[pl.ds(x, 1)] = chi[pl.ds(x, 1)]
+    over[pl.ds(plane, 1)] = chi[pl.ds(plane, 1)]
 
     def homeward(step):
-        @pl.when(step == 1)
+        @pl.when(step == 2)
         def _():
-            for j in (1, 2, 3):
+            for j in range(1, 8):
                 result(0, j).wait()
             for j in (1, 2, 3):
                 result(1, j).start()
-            for n in range(4):
-                for p in range(2):
-                    over_y[y, n, p] = over_x[n, p, y]
-
-        @pl.when(step == 3)
-        def _():
-            for j in (1, 2, 3):
-                result(1, j).wait()
-            result(2, 0).start()
-            for n in range(4):
-                for p in range(4):
-                    slots[z, n, p] = over_y[n, p, z]
-
-    scan(2, homeward)
+            for n in range(8):
+                slots[y, n] = over[n, y]
+
+    scan(place.across, homeward)
     tops[...] = jnp.concatenate([jnp.max(peak[m], axis=0, keepdims=True) for m in range(NT)], 0)
     pairs = [
         pltpu.make_async_remote_copy(
@@ -484,12 +491,13 @@
     for copy in pairs:
         copy.start()
     place.finish()
-    result(2, 0).wait()
+    for j in (1, 2, 3):
+        result(1, j).wait()
     i, j = iota((64, 64), 0), iota((64, 64), 1)
     across = own_ref[...]
     owner = jnp.sum(jnp.where(i == j, across, 0), axis=1, keepdims=True)
     rank = jnp.sum(jnp.where((j < i) & (across == owner), 1, 0), axis=1, keepdims=True)
-    where = owner // 16 * 16 + owner % 4 * 4 + owner // 4 % 4
+    where = owner % 4 * 8 + owner // 4
     choose = jnp.where(iota((64, 256), 1) == where * 8 + rank, 1.0, 0.0)
     out_ref[...] = jnp.dot(
         choose, slots[...].reshape(256, 128), preferred_element_type=F32, precision=lax.Precision.HIGHEST
@@ -503,25 +511,17 @@
 
 
 def handed_kernel(*refs):
-    sem = refs[6]
-    copies = [pltpu.make_async_copy(refs[n], refs[n + 3], sem.at[n]) for n in (1, 2)]
-    for n in range(4):
-        cut = pl.ds(4 * n, 4)
-        copies.append(pltpu.make_async_copy(refs[0].at[cut], refs[3].at[cut], sem.at[3 + n]))
-    for copy in copies:
-        copy.start()
-    for copy in copies:
-        copy.wait()
+    for n in range(3):
+        refs[n + 3][...] = refs[n][...]
 
 
 def handed(*arrays):
-    hbm = pl.BlockSpec(memory_space=pltpu.HBM)
+    vmem = pl.BlockSpec(memory_space=pltpu.VMEM)
     return pl.pallas_call(
         handed_kernel,
         out_shape=tuple(jax.ShapeDtypeStruct(a.shape, a.dtype) for a in arrays),
-        in_specs=[hbm] * 3,
-        out_specs=(hbm,) * 3,
-        scratch_shapes=[pltpu.SemaphoreType.DMA((7,))],
+        in_specs=[vmem] * 3,
+        out_specs=(vmem,) * 3,
         name="handed",
     )(*arrays)
 
@@ -569,18 +569,17 @@
             pltpu.VMEM((NT, 8, 128), F32),
             pltpu.VMEM((8, 128), I32),
             pltpu.SMEM((8, 128), I32),
-            pltpu.VMEM((4, 2, 4, 8, 128), F32),
-            pltpu.VMEM((4, 2, 4, 8, 128), F32),
-            pltpu.VMEM((4, 4, 2, 8, 128), F32),
-            pltpu.VMEM((2, 4, 4, 8, 128), F32),
+            pltpu.VMEM((8, 4, 8, 128), F32),
+            pltpu.VMEM((8, 4, 8, 128), F32),
+            pltpu.VMEM((4, 8, 8, 128), F32),
             pltpu.VMEM((NT, 128), F32),
             pltpu.VMEM((4, NT, 128), F32),
             dma((21,)),
             dma((2, 10)),
             dma((2, 32)),
             dma,
-            dma((3, 4)),
-            dma((3, 4)),
+            dma((2, 8)),
+            dma((2, 8)),
             dma((4,)),
             dma((4,)),
             dma((11,)),

time: 93.4 us -> 60 us (0.64); the launches traced: 92.3 us -> 59.9 us
  Pallas kernels: 91.5 us -> 59.3 us
    pallas_call x1, Pallas kernels: 33.9 us -> 2.27 us  [handed(): pl.pallas_call(handed_kernel, out_shape=tuple((jax.ShapeDtypeStruct(a.sha...]
where the time goes in v5:
time: 60 us; the launch traced here: 59.9 us
  Pallas kernels  59.3 us (99%)
  between operations  0.64 us (1%)
    pallas_call x1, Pallas kernels, body(): pl.pallas_call(kernel, out_shape=(jax.ShapeDtypeStruct((NT, 128, 128), F3...  57 us
    pallas_call x1, Pallas kernels, handed(): pl.pallas_call(handed_kernel, out_shape=tuple((jax.ShapeDtypeStruct(a.sha...  2.27 us

profile of v5, /device:TPU:0, one launch (start us, length us, event | category | flops | bytes accessed | tf_op | source)
XLA Modules:
  0.0 59.9 jit_solution(11799284234039471001)
XLA Ops:
  0.6 57.0 %search.1 = (f32[16,128,128]{2,1,0:T(8,128)}, f32[1,16]{1,0:T(1,128)}, f32[64,128]{1,0:T(8,128)}) custom-call(bf16[2,2,2,4096]{3,2,1,0:T(2,128)(2,1)} %bitcast.11, s32[1,64]{1,0:T(1,128)} %bitcast.12, s32[1,64]{1,0:T(1,128)} %bitcast.13, s32[1,64]{1,0:T(1,128)} %bitcast.14, s32[1,64]{1,0:T(1,128)} %bitcast.15, bf16[2,16,4096]{2,1,0:T(8,128)(2,1)} %tm_in.1, ...), custom_call_target="tpu_custom_call" | custom-call | tf_op jit(solution)/shard_map/search/pallas_call | solution.py:535
  57.6 2.3 %handed.1 = (f32[16,128,128]{2,1,0:T(8,128)}, f32[1,16]{1,0:T(1,128)}, f32[64,128]{1,0:T(8,128)}) custom-call(f32[16,128,128]{2,1,0:T(8,128)} %get-tuple-element.9.refs_0_, f32[1,16]{1,0:T(1,128)} %get-tuple-element.10.refs_1_, f32[64,128]{1,0:T(8,128)} %get-tuple-element.11.refs_2_), custom_call_target="tpu_custom_call" | custom-call | tf_op jit(solution)/shard_map/handed/pallas_call | solution.py:520

commit v6 on v5

--- a/solution.py
+++ b/solution.py
@@ -398,18 +398,11 @@
 
     def serve(member):
         asked = requests(place, held, wanted, meta, meta_sem, [member(k) for k in range(8)])
-
-        @pl.loop(0, 8)
-        def _(k):
+        for k in range(8):
             turn(held, rot_ref, turned, nat, member(k), k)
-
         asked.wait()
-
-        @pl.loop(0, 2)
-        def _(part):
-            for n in range(4):
-                slot = part * 4 + n
-                veto(w0_ref, far_ref, tn, meta, turned, masks, pick, weight, chi, slot, slot, member(slot))
+        for slot in range(8):
+            veto(w0_ref, far_ref, tn, meta, turned, masks, pick, weight, chi, slot, slot, member(slot))
 
     def scan(member, between):
         spread(nat, sre, sim)

time: 60 us -> 59.1 us (0.985)
  Pallas kernels: 59.3 us -> 58.3 us
    pallas_call x1, Pallas kernels: 57 us -> 56 us  [body(): pl.pallas_call(kernel, out_shape=(jax.ShapeDtypeStruct((NT, 128, 128), F3...]
where the time goes in v6:
time: 59.1 us; the launch traced here: 59 us
  Pallas kernels  58.3 us (99%)
  between operations  0.64 us (1%)
    pallas_call x1, Pallas kernels, body(): pl.pallas_call(kernel, out_shape=(jax.ShapeDtypeStruct((NT, 128, 128), F3...  56 us
    pallas_call x1, Pallas kernels, handed(): pl.pallas_call(handed_kernel, out_shape=tuple((jax.ShapeDtypeStruct(a.sha...  2.27 us

profile of v6, /device:TPU:0, one launch (start us, length us, event | category | flops | bytes accessed | tf_op | source)
XLA Modules:
  0.0 59.0 jit_solution(11758504288498746625)
XLA Ops:
  0.6 56.0 %search.1 = (f32[16,128,128]{2,1,0:T(8,128)}, f32[1,16]{1,0:T(1,128)}, f32[64,128]{1,0:T(8,128)}) custom-call(bf16[2,2,2,4096]{3,2,1,0:T(2,128)(2,1)} %bitcast.11, s32[1,64]{1,0:T(1,128)} %bitcast.12, s32[1,64]{1,0:T(1,128)} %bitcast.13, s32[1,64]{1,0:T(1,128)} %bitcast.14, s32[1,64]{1,0:T(1,128)} %bitcast.15, bf16[2,16,4096]{2,1,0:T(8,128)(2,1)} %tm_in.1, ...), custom_call_target="tpu_custom_call" | custom-call | tf_op jit(solution)/shard_map/search/pallas_call | solution.py:528
  56.7 2.3 %handed.1 = (f32[16,128,128]{2,1,0:T(8,128)}, f32[1,16]{1,0:T(1,128)}, f32[64,128]{1,0:T(8,128)}) custom-call(f32[16,128,128]{2,1,0:T(8,128)} %get-tuple-element.9.refs_0_, f32[1,16]{1,0:T(1,128)} %get-tuple-element.10.refs_1_, f32[64,128]{1,0:T(8,128)} %get-tuple-element.11.refs_2_), custom_call_target="tpu_custom_call" | custom-call | tf_op jit(solution)/shard_map/handed/pallas_call | solution.py:513
